TPU v7x, 1024 devices: a whole 4x8x16 slice. The times are simulated.
1024 devices in a mesh: mid: 128 (over y, z), off: 8 (over x, core).
Axes of the slice: x: 4, y: 8, z: 16, core: 2. Of those that a mesh axis runs over, the one named last changes fastest.
Arguments:
- traces: bfloat16 [131072, 512], P(('mid', 'off')), may hold values from -16 to 16
- kernels: bfloat16 [8, 512, 512], replicated, may hold values from -0.25 to 0.25
- send_list: int32 [128, 4, 4], P('mid'), may hold values from 0 to 7, as said below
- aper_slot: int32 [8, 131072], P(None, ('mid', 'off')), may hold values from 0 to 23, as said below
- aper_pattern: int32 [8, 131072], P(None, ('mid', 'off')), may hold values from 0 to 7
- trace_bin: int32 [131072], P(('mid', 'off')), may hold values from 0 to 7
- trace_count: int32 [131072], P(('mid', 'off')), may hold values from 5 to 8, as said below
Outputs:
- solution: float32 [1024, 64, 512], P('mid', 'off')
- residual: float32 [1024, 64, 512], P('mid', 'off')
Inputs may be any that keep to these rules, and one draw needn't show every extreme that they name: Each row send_list[i, k, :] holds 4 different cells of tile i. `aper_slot`: with r = j % 5, entry j of every list names one of the 8 own cells of the trace's tile when r == 0, and otherwise one of slots 8 + (r - 1) * 4 to 8 + r * 4 - 1, the cells that arrive from direction r - 1. Only the first trace_count[t] entries of a list are live.
All inputs are finite; a program needn't handle non-finite values.
Results may differ from a plain program's by a relative error of at most 0.015.
Values may be sent and summed in bfloat16 or wider, within the bound.
A program may use at most 32 MiB of HBM per device.

v0:
```python
import jax
import jax.numpy as jnp
from jax import lax
from jax.sharding import PartitionSpec as P

NOFF = 64
PATTERNS = 8
REACH = 2
APER = 8
ITERS = 2
CELLS = 8


smooth_weight = 2.0


def padded_2(x, sides, width):
    for axis, dim in sides:
        peers, length = (lax.axis_size(axis), x.shape[dim])
        up = [(i, (i + 1) % peers) for i in range(peers - 1)]
        down = [(j, i) for i, j in up]
        last = lax.slice_in_dim(x, length - width, length, axis=dim)
        first = lax.slice_in_dim(x, 0, width, axis=dim)
        before = lax.ppermute(last, axis, up)
        after = lax.ppermute(first, axis, down)
        x = jnp.concatenate([before, x, after], axis=dim)
    return x


def from_behind(x, axis, by):
    peers = lax.axis_size(axis)
    pairs = [(i, i + by) for i in range(peers) if 0 <= i + by < peers]
    return lax.ppermute(x, axis, pairs)


def direction_shift(course):
    return (course // 2 + 1) * (1 - 2 * (course % 2))


def offset_laplace(padded):
    return smooth_weight * (2.0 * padded[:, 1:-1] - padded[:, :-2] - padded[:, 2:])


def smoothing(field):
    padded = padded_2(field, (("off", 1),), 1)
    smoothed = offset_laplace(padded)
    return smoothed


def deliver(outgoing):
    arrived = [None] * (2 * REACH)
    for course in range(2 * REACH):
        arrived[course] = from_behind(outgoing[course], "mid", direction_shift(course))
    return arrived


def give_back(returning):
    landed = [None] * (2 * REACH)
    for course in range(2 * REACH):
        landed[course] = from_behind(returning[course], "mid", -direction_shift(course))
    return landed


def shards(traces, kernels, send_list, aper_slot, aper_pattern, trace_bin, trace_count):
    off_dev = NOFF // lax.axis_size("off")
    trace_rows = traces.shape[0]
    samples = traces.shape[1]
    chosen_cells = send_list[0]
    send_count = chosen_cells.shape[1]
    slot_count = CELLS + 2 * REACH * send_count
    live_mask = jnp.arange(APER, dtype=jnp.int32)[:, None] < trace_count[None, :]
    row_index = (aper_slot * off_dev + trace_bin[None, :]).reshape(-1)
    pattern_ids = jnp.arange(PATTERNS, dtype=jnp.int32)[:, None, None]
    chooser = ((aper_pattern[None] == pattern_ids) & live_mask[None]).astype(jnp.bfloat16)
    pick_rows = (
        aper_pattern * trace_rows + jnp.arange(trace_rows, dtype=jnp.int32)[None, :]
    ).reshape(-1)
    live_column = live_mask.reshape(-1, 1).astype(jnp.float32)

    def forward(field_bf):
        outgoing = [field_bf[chosen_cells[course]] for course in range(2 * REACH)]
        arrived = deliver(outgoing)
        slot_rows = jnp.concatenate([field_bf] + arrived, 0).reshape(-1, samples)
        blocks = slot_rows[row_index].reshape(APER, trace_rows, samples)
        pattern_sums = jnp.einsum(
            "pjt,jtn->ptn", chooser, blocks, preferred_element_type=jnp.float32
        ).astype(jnp.bfloat16)
        return jnp.einsum("ptn,pnm->tm", pattern_sums, kernels, preferred_element_type=jnp.float32)

    def adjoint(values_bf):
        spread = jnp.einsum(
            "tm,pnm->ptn", values_bf, kernels, preferred_element_type=jnp.float32
        ).reshape(-1, samples)
        entries = spread[pick_rows] * live_column
        slot_sums = (
            jnp.zeros((slot_count * off_dev, samples), jnp.float32).at[row_index].add(entries)
        )
        slot_sums = slot_sums.reshape(slot_count, off_dev, samples)
        returning = [
            slot_sums[CELLS + course * send_count : CELLS + (course + 1) * send_count]
            for course in range(2 * REACH)
        ]
        landed = give_back(returning)
        accumulated = slot_sums[:CELLS]
        for course in range(2 * REACH):
            accumulated = accumulated.at[chosen_cells[course]].add(landed[course])
        return accumulated

    def global_total(value):
        return lax.psum(value, ("mid", "off"))

    residual = adjoint(traces)
    direction = residual
    solution = jnp.zeros_like(residual)
    norm_now = global_total(jnp.sum(residual * residual))
    for iteration in range(ITERS):
        applied = adjoint(forward(direction.astype(jnp.bfloat16)).astype(jnp.bfloat16)) + smoothing(
            direction
        )
        step_size = norm_now / global_total(jnp.sum(direction * applied))
        solution = solution + step_size * direction
        residual = residual - step_size * applied
        if iteration + 1 < ITERS:
            norm_next = global_total(jnp.sum(residual * residual))
            direction = residual + norm_next / norm_now * direction
            norm_now = norm_next
    return (solution, residual)


def solution(mesh):
    in_specs = (
        P(("mid", "off"), None),
        P(),
        P("mid", None, None),
        P(None, ("mid", "off")),
        P(None, ("mid", "off")),
        P(("mid", "off")),
        P(("mid", "off")),
    )
    out_specs = (P("mid", "off", None), P("mid", "off", None))
    return jax.shard_map(shards, mesh=mesh, in_specs=in_specs, out_specs=out_specs, check_vma=False)
```

profile of v0, /device:TPU:1, one launch (start us, length us, event | category | flops | bytes accessed | tf_op | source)
XLA Modules:
  0.0 557.1 jit_solution(6167460166867394359)
XLA Ops:
  2.8 3.7 fusion.43
  6.5 11.1 %scatter_custom_fusion = f32[192,512]{1,0:T(8,128)S(1)} fusion(s32[1024]{0:T(1024)S(1)} %bitcast.112, f32[1024]{0:T(1024)S(1)} %get-tuple-element.34, f32[]{:T(128)} %constant.7.clone.1, f32[1024,512]{1,0:T(8,128)S(1)} %bitcast.107, s32[1024]{0:T(1024)S(1)} %broadcast_clamp_fusion.1), kind=kCustom, calls=%fused_computation.32 | custom fusion | flops 1048576 | bytes 2498564 | tf_op jit(solution)/shard_map/scatter-add | solution.py:96
  19.0 5.5 collective-permute-start.1
  25.7 6.4 %collective-permute-start.3 = (f32[4,8,512]{2,1,0:T(8,128)S(1)}, f32[4,8,512]{2,1,0:T(8,128)S(1)}, u32[]{:S(2)}, u32[]{:S(2)}) collective-permute-start(f32[4,8,512]{2,1,0:T(8,128)S(1)} %get-tuple-element.19), channel_id=1, source_target_pairs={{0,16},{8,24},{16,32},{24,40},{32,48},{40,56},{48,64},{56,72},{64,... | collective-permute-start | bytes 196616 | tf_op jit(solution)/shard_map/ppermute | solution.py:33
  35.9 5.2 collective-permute-start.4
  44.2 6.4 %collective-permute-start.6 = (bf16[4,8,512]{2,1,0:T(8,128)(2,1)S(1)}, bf16[4,8,512]{2,1,0:T(8,128)(2,1)S(1)}, u32[]{:S(2)}, u32[]{:S(2)}) collective-permute-start(bf16[4,8,512]{2,1,0:T(8,128)(2,1)S(1)} %gather_fusion.2), channel_id=1, source_target_pairs={{0,16},{8,24},{16,32},{24,40},{32,48},{40,56},{48,64},{56,72},{64,... | collective-permute-start | bytes 98312 | tf_op jit(solution)/shard_map/ppermute | solution.py:33
  52.5 4.8 collective-permute-start.8
  57.4 8.9 %collective-permute-start.9 = (f32[8,1,512]{2,1,0:T(1,128)S(1)}, f32[8,1,512]{2,1,0:T(1,128)}, u32[]{:S(2)}, u32[]{:S(2)}) collective-permute-start(f32[8,1,512]{2,1,0:T(1,128)S(1)} %get-tuple-element.28), channel_id=1, source_target_pairs={{1,0},{2,1},{3,2},{4,3},{5,4},{6,5},{7,6},{9,8},{10,9},{11,10},{12... | collective-permute-start | bytes 49160 | tf_op jit(solution)/shard_map/ppermute | solution.py:25
  66.3 4.0 gather_fusion.4
  71.1 5.7 %fusion.20 = f32[128,8,512]{2,0,1:T(8,128)S(1)} fusion(bf16[8,512,512]{2,1,0:T(8,128)(2,1)} %param.8, bf16[8,128,512]{2,0,1:T(8,128)(2,1)S(1)} %fusion.6), kind=kOutput, calls=%fused_computation.51 | convolution fusion | flops 1073807360 | bytes 7340032 | tf_op jit(solution)/shard_map/tm,pnm->ptn/dot_general | solution.py:91
  76.9 11.1 %scatter_custom_fusion.5 = f32[192,512]{1,0:T(8,128)S(1)} fusion(s32[1024]{0:T(1024)S(1)} %bitcast.114, f32[1024]{0:T(1024)S(1)} %get-tuple-element.34, f32[]{:T(128)} %constant.7.clone.1, f32[1024,512]{1,0:T(8,128)S(1)} %bitcast.109, s32[1024]{0:T(1024)S(1)} %broadcast_clamp_fusion.1), kind=kCustom, calls=%fused_computation.30 | custom fusion | flops 1048576 | bytes 2498564 | tf_op jit(solution)/shard_map/scatter-add | solution.py:96
  89.4 4.0 collective-permute-start.11
  94.7 5.8 %collective-permute-start.13 = (f32[4,8,512]{2,1,0:T(8,128)S(1)}, f32[4,8,512]{2,1,0:T(8,128)S(1)}, u32[]{:S(2)}, u32[]{:S(2)}) collective-permute-start(f32[4,8,512]{2,1,0:T(8,128)S(1)} %get-tuple-element.15), channel_id=1, source_target_pairs={{0,16},{8,24},{16,32},{24,40},{32,48},{40,56},{48,64},{56,72},{64,... | collective-permute-start | bytes 196616 | tf_op jit(solution)/shard_map/ppermute | solution.py:33
  104.8 136.7 %all-reduce = (f32[]{:T(128)}, f32[]{:T(128)}) all-reduce(f32[]{:T(128)} %get-tuple-element.3, f32[]{:T(128)} %get-tuple-element.2), channel_id=1, replica_groups=mesh['mid'=128,'off'=8] {'mid','off'}, use_global_device_ids=true, to_apply=%region_6.0 | all-reduce | flops 2 | bytes 16 | tf_op jit(solution)/shard_map/psum | solution.py:110
  243.4 119.3 %psum.30 = f32[]{:T(128)} all-reduce(f32[]{:T(128)} %multiply_reduce_fusion.1), channel_id=1, replica_groups=mesh['mid'=128,'off'=8] {'mid','off'}, use_global_device_ids=true, to_apply=%region_15.0 | all-reduce | flops 1 | bytes 8 | tf_op jit(solution)/shard_map/psum | solution.py:110
  366.8 3.7 collective-permute-start.14
  371.8 3.7 collective-permute-start.16
  377.5 4.8 collective-permute-start.18
  384.5 4.0 gather_fusion.9
  389.3 5.7 %fusion.23 = f32[128,8,512]{2,0,1:T(8,128)S(1)} fusion(bf16[8,512,512]{2,1,0:T(8,128)(2,1)} %param.8, bf16[8,128,512]{2,0,1:T(8,128)(2,1)S(1)} %fusion.7), kind=kOutput, calls=%fused_computation.52 | convolution fusion | flops 1073807360 | bytes 7340032 | tf_op jit(solution)/shard_map/tm,pnm->ptn/dot_general | solution.py:91
  395.1 11.2 %scatter_custom_fusion.10 = f32[192,512]{1,0:T(8,128)S(1)} fusion(s32[1024]{0:T(1024)} %bitcast.115, f32[1024]{0:T(1024)S(1)} %copy-done.6, f32[]{:T(128)} %constant.7.clone.1, f32[1024,512]{1,0:T(8,128)S(1)} %bitcast.108, s32[1024]{0:T(1024)S(1)} %copy-done.8), kind=kCustom, calls=%fused_computation.28 | custom fusion | flops 1048576 | bytes 2499072 | tf_op jit(solution)/shard_map/scatter-add | solution.py:96
  407.7 4.0 collective-permute-start.21
  413.0 5.8 %collective-permute-start.23 = (f32[4,8,512]{2,1,0:T(8,128)S(1)}, f32[4,8,512]{2,1,0:T(8,128)S(1)}, u32[]{:S(2)}, u32[]{:S(2)}) collective-permute-start(f32[4,8,512]{2,1,0:T(8,128)S(1)} %get-tuple-element.11), channel_id=1, source_target_pairs={{0,16},{8,24},{16,32},{24,40},{32,48},{40,56},{48,64},{56,72},{64,... | collective-permute-start | bytes 196616 | tf_op jit(solution)/shard_map/ppermute | solution.py:33
  423.0 132.0 %psum.31 = f32[]{:T(128)} all-reduce(f32[]{:T(128)} %multiply_reduce_fusion), channel_id=1, replica_groups=mesh['mid'=128,'off'=8] {'mid','off'}, use_global_device_ids=true, to_apply=%region_22.0 | all-reduce | flops 1 | bytes 8 | tf_op jit(solution)/shard_map/psum | solution.py:110
  (149 shorter events, 37.8 us)
Async XLA Ops:
  17.7 14.9 %collective-permute-start = (f32[4,8,512]{2,1,0:T(8,128)S(1)}, f32[4,8,512]{2,1,0:T(8,128)S(1)}, u32[]{:S(2)}, u32[]{:S(2)}) collective-permute-start(f32[4,8,512]{2,1,0:T(8,128)S(1)} %get-tuple-element.22), channel_id=1, source_target_pairs={{8,0},{16,8},{24,16},{32,24},{40,32},{48,40},{56,48},{64,56},{72,6... | collective-permute-start | bytes 196616 | tf_op jit(solution)/shard_map/ppermute | solution.py:33
  19.0 14.3 %collective-permute-start.1 = (f32[4,8,512]{2,1,0:T(8,128)S(1)}, f32[4,8,512]{2,1,0:T(8,128)S(1)}, u32[]{:S(2)}, u32[]{:S(2)}) collective-permute-start(f32[4,8,512]{2,1,0:T(8,128)S(1)} %get-tuple-element.21), channel_id=1, source_target_pairs={{0,8},{8,16},{16,24},{24,32},{32,40},{40,48},{48,56},{56,64},{64,7... | collective-permute-start | bytes 196616 | tf_op jit(solution)/shard_map/ppermute | solution.py:33
  24.4 9.5 %collective-permute-start.2 = (f32[4,8,512]{2,1,0:T(8,128)S(1)}, f32[4,8,512]{2,1,0:T(8,128)S(1)}, u32[]{:S(2)}, u32[]{:S(2)}) collective-permute-start(f32[4,8,512]{2,1,0:T(8,128)S(1)} %get-tuple-element.20), channel_id=1, source_target_pairs={{16,0},{24,8},{32,16},{40,24},{48,32},{56,40},{64,48},{72,56},{80,... | collective-permute-start | bytes 196616 | tf_op jit(solution)/shard_map/ppermute | solution.py:33
  25.7 8.9 %collective-permute-start.3 = (f32[4,8,512]{2,1,0:T(8,128)S(1)}, f32[4,8,512]{2,1,0:T(8,128)S(1)}, u32[]{:S(2)}, u32[]{:S(2)}) collective-permute-start(f32[4,8,512]{2,1,0:T(8,128)S(1)} %get-tuple-element.19), channel_id=1, source_target_pairs={{0,16},{8,24},{16,32},{24,40},{32,48},{40,56},{48,64},{56,72},{64,... | collective-permute-start | bytes 196616 | tf_op jit(solution)/shard_map/ppermute | solution.py:33
  35.9 21.4 %collective-permute-start.4 = (bf16[4,8,512]{2,1,0:T(8,128)(2,1)S(1)}, bf16[4,8,512]{2,1,0:T(8,128)(2,1)S(1)}, u32[]{:S(2)}, u32[]{:S(2)}) collective-permute-start(bf16[4,8,512]{2,1,0:T(8,128)(2,1)S(1)} %gather_fusion), channel_id=1, source_target_pairs={{0,8},{8,16},{16,24},{24,32},{32,40},{40,48},{48,56},{56,64},{64,7... | collective-permute-start | bytes 98312 | tf_op jit(solution)/shard_map/ppermute | solution.py:33
  42.4 23.9 %collective-permute-start.5 = (bf16[4,8,512]{2,1,0:T(8,128)(2,1)S(1)}, bf16[4,8,512]{2,1,0:T(8,128)(2,1)S(1)}, u32[]{:S(2)}, u32[]{:S(2)}) collective-permute-start(bf16[4,8,512]{2,1,0:T(8,128)(2,1)S(1)} %gather_fusion.1), channel_id=1, source_target_pairs={{8,0},{16,8},{24,16},{32,24},{40,32},{48,40},{56,48},{64,56},{72,6... | collective-permute-start | bytes 98312 | tf_op jit(solution)/shard_map/ppermute | solution.py:33
  44.2 22.0 %collective-permute-start.6 = (bf16[4,8,512]{2,1,0:T(8,128)(2,1)S(1)}, bf16[4,8,512]{2,1,0:T(8,128)(2,1)S(1)}, u32[]{:S(2)}, u32[]{:S(2)}) collective-permute-start(bf16[4,8,512]{2,1,0:T(8,128)(2,1)S(1)} %gather_fusion.2), channel_id=1, source_target_pairs={{0,16},{8,24},{16,32},{24,40},{32,48},{40,56},{48,64},{56,72},{64,... | collective-permute-start | bytes 98312 | tf_op jit(solution)/shard_map/ppermute | solution.py:33
  51.2 15.1 %collective-permute-start.7 = (bf16[4,8,512]{2,1,0:T(8,128)(2,1)S(1)}, bf16[4,8,512]{2,1,0:T(8,128)(2,1)S(1)}, u32[]{:S(2)}, u32[]{:S(2)}) collective-permute-start(bf16[4,8,512]{2,1,0:T(8,128)(2,1)S(1)} %gather_fusion.3), channel_id=1, source_target_pairs={{16,0},{24,8},{32,16},{40,24},{48,32},{56,40},{64,48},{72,56},{80,... | collective-permute-start | bytes 98312 | tf_op jit(solution)/shard_map/ppermute | solution.py:33
  52.5 42.2 %collective-permute-start.8 = (f32[8,1,512]{2,1,0:T(1,128)}, f32[8,1,512]{2,1,0:T(1,128)}, u32[]{:S(2)}, u32[]{:S(2)}) collective-permute-start(f32[8,1,512]{2,1,0:T(1,128)} %get-tuple-element.27), channel_id=1, source_target_pairs={{0,1},{1,2},{2,3},{3,4},{4,5},{5,6},{6,7},{8,9},{9,10},{10,11},{11... | collective-permute-start | bytes 49160 | tf_op jit(solution)/shard_map/ppermute | solution.py:24
  57.4 43.2 %collective-permute-start.9 = (f32[8,1,512]{2,1,0:T(1,128)S(1)}, f32[8,1,512]{2,1,0:T(1,128)}, u32[]{:S(2)}, u32[]{:S(2)}) collective-permute-start(f32[8,1,512]{2,1,0:T(1,128)S(1)} %get-tuple-element.28), channel_id=1, source_target_pairs={{1,0},{2,1},{3,2},{4,3},{5,4},{6,5},{7,6},{9,8},{10,9},{11,10},{12... | collective-permute-start | bytes 49160 | tf_op jit(solution)/shard_map/ppermute | solution.py:25
  88.1 13.2 %collective-permute-start.10 = (f32[4,8,512]{2,1,0:T(8,128)S(1)}, f32[4,8,512]{2,1,0:T(8,128)S(1)}, u32[]{:S(2)}, u32[]{:S(2)}) collective-permute-start(f32[4,8,512]{2,1,0:T(8,128)S(1)} %get-tuple-element.18), channel_id=1, source_target_pairs={{8,0},{16,8},{24,16},{32,24},{40,32},{48,40},{56,48},{64,56},{72,6... | collective-permute-start | bytes 196616 | tf_op jit(solution)/shard_map/ppermute | solution.py:33
  89.4 12.6 %collective-permute-start.11 = (f32[4,8,512]{2,1,0:T(8,128)S(1)}, f32[4,8,512]{2,1,0:T(8,128)S(1)}, u32[]{:S(2)}, u32[]{:S(2)}) collective-permute-start(f32[4,8,512]{2,1,0:T(8,128)S(1)} %get-tuple-element.17), channel_id=1, source_target_pairs={{0,8},{8,16},{16,24},{24,32},{32,40},{40,48},{48,56},{56,64},{64,7... | collective-permute-start | bytes 196616 | tf_op jit(solution)/shard_map/ppermute | solution.py:33
  93.4 9.3 %collective-permute-start.12 = (f32[4,8,512]{2,1,0:T(8,128)S(1)}, f32[4,8,512]{2,1,0:T(8,128)S(1)}, u32[]{:S(2)}, u32[]{:S(2)}) collective-permute-start(f32[4,8,512]{2,1,0:T(8,128)S(1)} %get-tuple-element.16), channel_id=1, source_target_pairs={{16,0},{24,8},{32,16},{40,24},{48,32},{56,40},{64,48},{72,56},{80,... | collective-permute-start | bytes 196616 | tf_op jit(solution)/shard_map/ppermute | solution.py:33
  94.7 8.7 %collective-permute-start.13 = (f32[4,8,512]{2,1,0:T(8,128)S(1)}, f32[4,8,512]{2,1,0:T(8,128)S(1)}, u32[]{:S(2)}, u32[]{:S(2)}) collective-permute-start(f32[4,8,512]{2,1,0:T(8,128)S(1)} %get-tuple-element.15), channel_id=1, source_target_pairs={{0,16},{8,24},{16,32},{24,40},{32,48},{40,56},{48,64},{56,72},{64,... | collective-permute-start | bytes 196616 | tf_op jit(solution)/shard_map/ppermute | solution.py:33
  366.8 15.4 %collective-permute-start.14 = (bf16[4,8,512]{2,1,0:T(8,128)(2,1)S(1)}, bf16[4,8,512]{2,1,0:T(8,128)(2,1)S(1)}, u32[]{:S(2)}, u32[]{:S(2)}) collective-permute-start(bf16[4,8,512]{2,1,0:T(8,128)(2,1)S(1)} %gather_fusion.5), channel_id=1, source_target_pairs={{0,8},{8,16},{16,24},{24,32},{32,40},{40,48},{48,56},{56,64},{64,7... | collective-permute-start | bytes 98312 | tf_op jit(solution)/shard_map/ppermute | solution.py:33
  370.5 13.9 %collective-permute-start.15 = (bf16[4,8,512]{2,1,0:T(8,128)(2,1)S(1)}, bf16[4,8,512]{2,1,0:T(8,128)(2,1)S(1)}, u32[]{:S(2)}, u32[]{:S(2)}) collective-permute-start(bf16[4,8,512]{2,1,0:T(8,128)(2,1)S(1)} %gather_fusion.6), channel_id=1, source_target_pairs={{8,0},{16,8},{24,16},{32,24},{40,32},{48,40},{56,48},{64,56},{72,6... | collective-permute-start | bytes 98312 | tf_op jit(solution)/shard_map/ppermute | solution.py:33
  371.8 12.6 %collective-permute-start.16 = (bf16[4,8,512]{2,1,0:T(8,128)(2,1)S(1)}, bf16[4,8,512]{2,1,0:T(8,128)(2,1)S(1)}, u32[]{:S(2)}, u32[]{:S(2)}) collective-permute-start(bf16[4,8,512]{2,1,0:T(8,128)(2,1)S(1)} %gather_fusion.7), channel_id=1, source_target_pairs={{0,16},{8,24},{16,32},{24,40},{32,48},{40,56},{48,64},{56,72},{64,... | collective-permute-start | bytes 98312 | tf_op jit(solution)/shard_map/ppermute | solution.py:33
  375.5 8.9 %collective-permute-start.17 = (bf16[4,8,512]{2,1,0:T(8,128)(2,1)S(1)}, bf16[4,8,512]{2,1,0:T(8,128)(2,1)S(1)}, u32[]{:S(2)}, u32[]{:S(2)}) collective-permute-start(bf16[4,8,512]{2,1,0:T(8,128)(2,1)S(1)} %gather_fusion.8), channel_id=1, source_target_pairs={{16,0},{24,8},{32,16},{40,24},{48,32},{56,40},{64,48},{72,56},{80,... | collective-permute-start | bytes 98312 | tf_op jit(solution)/shard_map/ppermute | solution.py:33
  377.5 35.5 %collective-permute-start.18 = (f32[8,1,512]{2,1,0:T(1,128)}, f32[8,1,512]{2,1,0:T(1,128)}, u32[]{:S(2)}, u32[]{:S(2)}) collective-permute-start(f32[8,1,512]{2,1,0:T(1,128)} %get-tuple-element.25), channel_id=1, source_target_pairs={{0,1},{1,2},{2,3},{3,4},{4,5},{5,6},{6,7},{8,9},{9,10},{10,11},{11... | collective-permute-start | bytes 49160 | tf_op jit(solution)/shard_map/ppermute | solution.py:24
  382.2 36.6 %collective-permute-start.19 = (f32[8,1,512]{2,1,0:T(1,128)}, f32[8,1,512]{2,1,0:T(1,128)}, u32[]{:S(2)}, u32[]{:S(2)}) collective-permute-start(f32[8,1,512]{2,1,0:T(1,128)} %get-tuple-element.26), channel_id=1, source_target_pairs={{1,0},{2,1},{3,2},{4,3},{5,4},{6,5},{7,6},{9,8},{10,9},{11,10},{12... | collective-permute-start | bytes 49160 | tf_op jit(solution)/shard_map/ppermute | solution.py:25
  406.4 13.2 %collective-permute-start.20 = (f32[4,8,512]{2,1,0:T(8,128)S(1)}, f32[4,8,512]{2,1,0:T(8,128)S(1)}, u32[]{:S(2)}, u32[]{:S(2)}) collective-permute-start(f32[4,8,512]{2,1,0:T(8,128)S(1)} %get-tuple-element.14), channel_id=1, source_target_pairs={{8,0},{16,8},{24,16},{32,24},{40,32},{48,40},{56,48},{64,56},{72,6... | collective-permute-start | bytes 196616 | tf_op jit(solution)/shard_map/ppermute | solution.py:33
  407.7 12.6 %collective-permute-start.21 = (f32[4,8,512]{2,1,0:T(8,128)S(1)}, f32[4,8,512]{2,1,0:T(8,128)S(1)}, u32[]{:S(2)}, u32[]{:S(2)}) collective-permute-start(f32[4,8,512]{2,1,0:T(8,128)S(1)} %get-tuple-element.13), channel_id=1, source_target_pairs={{0,8},{8,16},{16,24},{24,32},{32,40},{40,48},{48,56},{56,64},{64,7... | collective-permute-start | bytes 196616 | tf_op jit(solution)/shard_map/ppermute | solution.py:33
  411.7 9.3 %collective-permute-start.22 = (f32[4,8,512]{2,1,0:T(8,128)S(1)}, f32[4,8,512]{2,1,0:T(8,128)S(1)}, u32[]{:S(2)}, u32[]{:S(2)}) collective-permute-start(f32[4,8,512]{2,1,0:T(8,128)S(1)} %get-tuple-element.12), channel_id=1, source_target_pairs={{16,0},{24,8},{32,16},{40,24},{48,32},{56,40},{64,48},{72,56},{80,... | collective-permute-start | bytes 196616 | tf_op jit(solution)/shard_map/ppermute | solution.py:33
  413.0 8.7 %collective-permute-start.23 = (f32[4,8,512]{2,1,0:T(8,128)S(1)}, f32[4,8,512]{2,1,0:T(8,128)S(1)}, u32[]{:S(2)}, u32[]{:S(2)}) collective-permute-start(f32[4,8,512]{2,1,0:T(8,128)S(1)} %get-tuple-element.11), channel_id=1, source_target_pairs={{0,16},{8,24},{16,32},{24,40},{32,48},{40,56},{48,64},{56,72},{64,... | collective-permute-start | bytes 196616 | tf_op jit(solution)/shard_map/ppermute | solution.py:33
  (28 other events, 667.2 us)
where the time goes:
time: 563 us; the launch traced here: 557 us
  blocking collectives  388 us (69%)
  starting transfers between devices  84 us (15%)
  other arithmetic  48 us (9%)
  matrix products  16.7 us (3%)
  local copies, waits for them, and re-layouts  14.5 us (3%)
  between operations  5.89 us (1%)
    psum x3, blocking collectives, global_total(): return lax.psum(value, ('mid', 'off'))  388 us
    ppermute x20, starting transfers between devices, from_behind(): return lax.ppermute(x, axis, pairs)  63.4 us
    scatter-add x3, other arithmetic, adjoint(): jnp.zeros((slot_count * off_dev, samples), jnp.float32).at[row_index]  33.5 us
    dot_general x3, matrix products, adjoint(): jnp.einsum('tm,pnm->ptn', values_bf, kernels, preferred_element_type=jnp....  15.1 us
  transfers between devices with their start and end apart: 24, of which 0 were waited for; matrix products, arithmetic and copies ran while one was open for 10% of the time, Pallas kernels for 0%

commit v1 on v0

v1 whole, which is shorter than its diff:
```python
import functools

import jax
import jax.numpy as jnp
from jax import lax
from jax.experimental import pallas as pl
from jax.experimental.pallas import tpu as pltpu
from jax.sharding import PartitionSpec as P

MESH = pl.DeviceIdType.MESH
PATTERNS = 8
APER = 8
CELLS = 8
SEND = 4
DIRS = 4
BINS = 8
OWN = CELLS * BINS
PART = SEND * BINS
AWAY = DIRS * PART
ROWS = OWN + AWAY
CHUNKS = 2
SHIFTS = (1, -1, 2, -2)
FAR_FIRST = (2, 3, 0, 1)
smooth_weight = 2.0
F32 = jnp.float32
BF16 = jnp.bfloat16


def dot(a, b):
    return jnp.dot(a, b, preferred_element_type=F32)


def dot_t(a, b):
    return lax.dot_general(a, b, (((1,), (1,)), ((), ())), preferred_element_type=F32)


def by_lanes(x):
    rows, n = x.shape
    x = x.reshape(rows // 8, 8, n).sum(0)
    x = sum(x[:, i : i + 128] for i in range(0, n, 128))
    return jnp.sum(x, axis=0, keepdims=True)


def body(
    sizes,
    traces_ref,
    kernels_ref,
    send_ref,
    slot_ref,
    pattern_ref,
    bin_ref,
    count_ref,
    solution_ref,
    residual_ref,
    moveout,
    pick,
    spread_to,
    spread,
    own,
    back_send,
    back_land,
    slots,
    ahead_send,
    field0,
    field1,
    smooth,
    edge_send,
    edge_land,
    totals,
    total_send,
    total_a,
    total_b,
    total_c,
    load_sem,
    back_ssem,
    back_rsem,
    ahead_ssem,
    ahead_rsem,
    edge_ssem,
    edge_rsem,
    total_ssem,
    total_rsem,
):
    n_mid, n_off, n_z = sizes
    n_y = n_mid // n_z
    samples = moveout.shape[2]
    trace_rows = traces_ref.shape[0]
    width = samples // CHUNKS
    mid = lax.axis_index("mid")
    off = lax.axis_index("off")
    row_y = lax.div(mid, n_z)
    col_z = lax.rem(mid, n_z)

    def tile_at(shift):
        return lax.rem(mid + (shift + n_mid), n_mid)

    tiles_to = [tile_at(s) for s in SHIFTS]
    tiles_back = [tile_at(-s) for s in SHIFTS]
    off_peers = [lax.rem(off + d, n_off) for d in range(1, n_off)]
    z_peers = [row_y * n_z + lax.rem(col_z + d, n_z) for d in range(1, n_z)]
    y_peers = [lax.rem(row_y + d, n_y) * n_z + col_z for d in range(1, n_y)]

    loads = [
        pltpu.make_async_copy(kernels_ref.at[p], moveout.at[p], load_sem.at[p]) for p in range(PATTERNS)
    ]
    for load in loads:
        load.start()

    barrier = pltpu.get_barrier_semaphore()
    greeted = 0
    for tile in tiles_to + z_peers + y_peers:
        pl.semaphore_signal(barrier, inc=1, device_id=(tile, off), device_id_type=MESH)
        greeted += 1
    for peer in off_peers:
        pl.semaphore_signal(barrier, inc=1, device_id=(mid, peer), device_id_type=MESH)
        greeted += 1

    slot = slot_ref[...]
    live = lax.broadcasted_iota(jnp.int32, slot.shape, 0) < count_ref[...].reshape(1, trace_rows)
    for k in range(DIRS):
        source = mid - SHIFTS[k]
        here = (source >= 0) & (source < n_mid)
        inside = (slot >= CELLS + k * SEND) & (slot < CELLS + (k + 1) * SEND)
        live = live & (jnp.logical_not(inside) | here)
    code = pattern_ref[...] * ROWS + slot * BINS + bin_ref[...].reshape(1, trace_rows)
    code = jnp.where(live, code, -1)
    row_id = lax.broadcasted_iota(jnp.int32, (ROWS, trace_rows), 0)
    for p in range(PATTERNS):
        count = jnp.zeros((ROWS, trace_rows), F32)
        for j in range(APER):
            count = count + jnp.where(code[j : j + 1, :] - p * ROWS == row_id, 1.0, 0.0)
        spread_to[:, p * trace_rows : (p + 1) * trace_rows] = count.astype(BF16)
        pick[p * trace_rows : (p + 1) * trace_rows, :] = count.T.astype(BF16)

    entry = lax.broadcasted_iota(jnp.int32, (OWN, AWAY), 1)
    listed = jnp.zeros((OWN, AWAY), jnp.int32)
    for k in range(DIRS):
        for m in range(SEND):
            listed = jnp.where(entry // BINS == k * SEND + m, send_ref[0, k, m], listed)
    place = listed * BINS + entry % BINS
    land_f32 = jnp.where(place == lax.broadcasted_iota(jnp.int32, (OWN, AWAY), 0), 1.0, 0.0)
    land_at = land_f32.astype(BF16)
    take_from = land_f32.T.astype(BF16)

    def cols(c):
        return slice(c * width, (c + 1) * width)

    def back_copy(turn, c, k):
        part = pl.ds(k * PART, PART)
        return pltpu.make_async_remote_copy(
            src_ref=back_send.at[turn, c, part, :],
            dst_ref=back_land.at[turn, c, part, :],
            send_sem=back_ssem.at[turn, c],
            recv_sem=back_rsem.at[turn, c],
            device_id=(tiles_back[k], off),
            device_id_type=MESH,
        )

    def ahead_copy(turn, c, k):
        return pltpu.make_async_remote_copy(
            src_ref=ahead_send.at[turn, c, pl.ds(k * PART, PART), :],
            dst_ref=slots.at[turn, c, pl.ds(OWN + k * PART, PART), :],
            send_sem=ahead_ssem.at[turn, c],
            recv_sem=ahead_rsem.at[turn, c],
            device_id=(tiles_to[k], off),
            device_id_type=MESH,
        )

    def edge_copy(turn, side):
        step = 1 - 2 * side
        return pltpu.make_async_remote_copy(
            src_ref=edge_send.at[turn, side],
            dst_ref=edge_land.at[turn, side],
            send_sem=edge_ssem.at[turn, side],
            recv_sem=edge_rsem.at[turn, side],
            device_id=(mid, lax.rem(off + step + n_off, n_off)),
            device_id_type=MESH,
        )

    def await_bytes(ref, sem):
        pltpu.make_async_copy(ref, ref, sem).wait()

    def adjoint_chunk(turn, c, values, first=False):
        for p in range(PATTERNS):
            if first and c == 0:
                loads[p].wait()
            part = dot_t(values, moveout[p, cols(c), :])
            spread[p * trace_rows : (p + 1) * trace_rows, :] = part.astype(BF16)
        sums = dot(spread_to[...], spread[...])
        own[c] = sums[:OWN]
        back_send[turn, c] = sums[OWN:].astype(BF16)
        if first and c == 0:
            pl.semaphore_wait(barrier, greeted)
        for k in FAR_FIRST:
            back_copy(turn, c, k).start()

    def landed(turn, c):
        await_bytes(back_land.at[turn, c], back_rsem.at[turn, c])
        return own[c] + dot(land_at, back_land[turn, c])

    def ahead_chunk(turn, c, part):
        rounded = part.astype(BF16)
        ahead_send[turn, c] = dot(take_from, rounded).astype(BF16)
        for k in FAR_FIRST:
            ahead_copy(turn, c, k).start()
        slots[turn, c, :OWN, :] = rounded

    def send_edges(turn, field):
        cube = field[...].reshape(CELLS, BINS, samples)
        edge_send[turn, 0] = cube[:, BINS - 1, :]
        edge_send[turn, 1] = cube[:, 0, :]
        for side in range(2):
            edge_copy(turn, side).start()

    def smoothed(turn, field):
        for side in range(2):
            await_bytes(edge_land.at[turn, side], edge_rsem.at[turn, side])
        before = jnp.where(off == 0, 0.0, edge_land[turn, 0])
        after = jnp.where(off == n_off - 1, 0.0, edge_land[turn, 1])
        cube = field[...].reshape(CELLS, BINS, samples)
        padded = jnp.concatenate([before[:, None, :], cube, after[:, None, :]], axis=1)
        out = smooth_weight * (2.0 * cube - padded[:, :-2] - padded[:, 2:])
        return out.reshape(OWN, samples)

    def forward(turn):
        out = jnp.zeros((trace_rows, samples), F32)
        for c in range(CHUNKS):
            await_bytes(slots.at[turn, c, pl.ds(OWN, AWAY), :], ahead_rsem.at[turn, c])
            sums = dot(pick[...], slots[turn, c]).astype(BF16)
            for p in range(PATTERNS):
                out = out + dot(sums[p * trace_rows : (p + 1) * trace_rows], moveout[p, cols(c), :])
        return out

    def total_copies(turn, stage):
        land, where = stages[stage]
        return [
            pltpu.make_async_remote_copy(
                src_ref=total_send.at[turn, stage],
                dst_ref=land.at[turn, d],
                send_sem=total_ssem.at[turn, stage],
                recv_sem=total_rsem.at[turn, stage],
                device_id=device,
                device_id_type=MESH,
            )
            for d, device in enumerate(where)
        ]

    stages = [
        (total_a, [(mid, peer) for peer in off_peers]),
        (total_b, [(tile, off) for tile in z_peers]),
        (total_c, [(tile, off) for tile in y_peers]),
    ]

    def total_start(turn, stage, mine):
        total_send[turn, stage] = mine
        for copy in total_copies(turn, stage):
            copy.start()

    def total_end(turn, stage):
        land = stages[stage][0]
        await_bytes(land.at[turn], total_rsem.at[turn, stage])
        return total_send[turn, stage] + jnp.sum(land[turn], axis=0)

    values = traces_ref[...]
    for c in range(CHUNKS):
        adjoint_chunk(0, c, values, first=True)
    norm = jnp.zeros((1, 128), F32)
    for c in range(CHUNKS):
        part = landed(0, c)
        ahead_chunk(0, c, part)
        field0[:, cols(c)] = part
        norm = norm + by_lanes(part * part)

    for turn, field in ((0, field0), (1, field1)):
        send_edges(turn, field)
        smooth[...] = smoothed(turn, field)
        cross = by_lanes(field[...] * smooth[...])
        values = forward(turn).astype(BF16)
        heard = values.astype(F32)
        totals[0:1, :] = norm
        totals[1:2, :] = by_lanes(heard * heard) + cross
        totals[2:8, :] = jnp.zeros((6, 128), F32)
        total_start(turn, 0, totals[...])
        for c in range(CHUNKS):
            adjoint_chunk(turn + 1, c, values)
            if c < 2:
                total_start(turn, c + 1, total_end(turn, c))
        sums = jnp.sum(total_end(turn, 2), axis=1, keepdims=True)
        if turn == 0:
            norm_0 = sums[0:1, :]
            step_0 = norm_0 / sums[1:2, :]
            norm = jnp.zeros((1, 128), F32)
            for c in range(CHUNKS):
                part = field0[:, cols(c)] - step_0 * (landed(1, c) + smooth[:, cols(c)])
                ahead_chunk(1, c, part)
                field1[:, cols(c)] = part
                norm = norm + by_lanes(part * part)
        else:
            norm_1 = sums[0:1, :]
            ratio = norm_1 / norm_0
            step_1 = norm_1 / (sums[1:2, :] - ratio * (norm_1 / step_0))
            older = step_1 * ratio
            for c in range(CHUNKS):
                r, q = field0[:, cols(c)], field1[:, cols(c)]
                image = landed(2, c) + smooth[:, cols(c)]
                cube = (CELLS, BINS, width)
                solution_ref[:, :, cols(c)] = ((step_0 + older) * r + step_1 * q).reshape(cube)
                residual_ref[:, :, cols(c)] = (q - step_1 * image - (older / step_0) * (r - q)).reshape(cube)

    for turn in range(3):
        for c in range(CHUNKS):
            await_bytes(back_send.at[turn, c], back_ssem.at[turn, c])
    for turn in range(2):
        for c in range(CHUNKS):
            await_bytes(ahead_send.at[turn, c], ahead_ssem.at[turn, c])
        for side in range(2):
            await_bytes(edge_send.at[turn, side], edge_ssem.at[turn, side])
        for stage in range(3):
            await_bytes(stages[stage][0].at[turn], total_ssem.at[turn, stage])


def shards(sizes, traces, kernels, send_list, aper_slot, aper_pattern, trace_bin, trace_count):
    n_mid, n_off, n_z = sizes
    n_y = n_mid // n_z
    trace_rows, samples = traces.shape
    width = samples // CHUNKS
    vmem = pl.BlockSpec(memory_space=pltpu.VMEM)
    shape = jax.ShapeDtypeStruct((CELLS, BINS, samples), F32)
    return pl.pallas_call(
        functools.partial(body, sizes),
        out_shape=(shape, shape),
        in_specs=[
            vmem,
            pl.BlockSpec(memory_space=pl.ANY),
            pl.BlockSpec(memory_space=pltpu.SMEM),
            vmem,
            vmem,
            vmem,
            vmem,
        ],
        out_specs=(vmem, vmem),
        scratch_shapes=[
            pltpu.VMEM((PATTERNS, samples, samples), BF16),
            pltpu.VMEM((PATTERNS * trace_rows, ROWS), BF16),
            pltpu.VMEM((ROWS, PATTERNS * trace_rows), BF16),
            pltpu.VMEM((PATTERNS * trace_rows, width), BF16),
            pltpu.VMEM((CHUNKS, OWN, width), F32),
            pltpu.VMEM((3, CHUNKS, AWAY, width), BF16),
            pltpu.VMEM((3, CHUNKS, AWAY, width), BF16),
            pltpu.VMEM((2, CHUNKS, ROWS, width), BF16),
            pltpu.VMEM((2, CHUNKS, AWAY, width), BF16),
            pltpu.VMEM((OWN, samples), F32),
            pltpu.VMEM((OWN, samples), F32),
            pltpu.VMEM((OWN, samples), F32),
            pltpu.VMEM((2, 2, CELLS, samples), F32),
            pltpu.VMEM((2, 2, CELLS, samples), F32),
            pltpu.VMEM((8, 128), F32),
            pltpu.VMEM((2, 3, 8, 128), F32),
            pltpu.VMEM((2, n_off - 1, 8, 128), F32),
            pltpu.VMEM((2, n_z - 1, 8, 128), F32),
            pltpu.VMEM((2, n_y - 1, 8, 128), F32),
            pltpu.SemaphoreType.DMA((PATTERNS,)),
            pltpu.SemaphoreType.DMA((3, CHUNKS)),
            pltpu.SemaphoreType.DMA((3, CHUNKS)),
            pltpu.SemaphoreType.DMA((2, CHUNKS)),
            pltpu.SemaphoreType.DMA((2, CHUNKS)),
            pltpu.SemaphoreType.DMA((2, 2)),
            pltpu.SemaphoreType.DMA((2, 2)),
            pltpu.SemaphoreType.DMA((2, 3)),
            pltpu.SemaphoreType.DMA((2, 3)),
        ],
        compiler_params=pltpu.CompilerParams(
            collective_id=0, has_side_effects=True, vmem_limit_bytes=40 * 2**20
        ),
        name="inversion",
    )(traces, kernels, send_list, aper_slot, aper_pattern, trace_bin, trace_count)


def solution(mesh):
    n_mid, n_off = mesh.shape["mid"], mesh.shape["off"]
    n_z = 16 if n_mid % 16 == 0 else 4
    in_specs = (
        P(("mid", "off"), None),
        P(),
        P("mid", None, None),
        P(None, ("mid", "off")),
        P(None, ("mid", "off")),
        P(("mid", "off")),
        P(("mid", "off")),
    )
    out_specs = (P("mid", "off", None), P("mid", "off", None))
    return jax.shard_map(
        functools.partial(shards, (n_mid, n_off, n_z)),
        mesh=mesh,
        in_specs=in_specs,
        out_specs=out_specs,
        check_vma=False,
    )
```

time: 563 us -> 82.5 us (0.15)
  the two profiles are of different devices: /device:TPU:1 before, /device:TPU:2 now
where the time goes in v1:
time: 82.5 us; the launch traced here: 82.2 us
  Pallas kernels  73.8 us (89%)
  local copies, waits for them, and re-layouts  7.76 us (9%)
    pallas_call x1, Pallas kernels, shards(): pl.pallas_call(functools.partial(body, sizes), out_shape=(shape, shape),...  73.8 us
    unnamed x16, local copies, waits for them, and re-layouts  7.76 us

profile of v1, /device:TPU:2, one launch (start us, length us, event | category | flops | bytes accessed | tf_op | source)
XLA Modules:
  0.0 82.2 jit_solution(15281788523173058382)
XLA Ops:
  0.6 0.0 copy-start
  0.6 2.2 %copy-done = bf16[8,512,512]{2,1,0:T(8,128)(2,1)S(1)} copy-done((bf16[8,512,512]{2,1,0:T(8,128)(2,1)S(1)}, bf16[8,512,512]{2,1,0:T(8,128)(2,1)}, u32[]{:S(2)}) %copy-start) | copy-done | bytes 4194328
  2.8 0.0 copy-start.1
  2.8 0.9 %copy-done.1 = bf16[128,512]{1,0:T(8,128)(2,1)S(1)} copy-done((bf16[128,512]{1,0:T(8,128)(2,1)S(1)}, bf16[128,512]{1,0:T(8,128)(2,1)}, u32[]{:S(2)}) %copy-start.1) | copy-done | bytes 131096
  3.7 0.0 copy-start.2
  3.7 0.7 copy-done.2
  4.4 0.0 copy-start.3
  4.4 0.7 copy-done.3
  5.1 0.0 copy-start.4
  5.1 0.7 copy-done.4
  5.8 0.0 copy-start.5
  5.8 0.7 copy-done.5
  6.4 0.0 copy-start.6
  6.4 0.7 copy-done.6
  7.1 73.8 %inversion.1 = (f32[8,8,512]{2,1,0:T(8,128)S(1)}, f32[8,8,512]{2,1,0:T(8,128)S(1)}) custom-call(bf16[128,512]{1,0:T(8,128)(2,1)S(1)} %copy-done.1, bf16[8,512,512]{2,1,0:T(8,128)(2,1)S(1)} %copy-done, s32[1,4,4]{2,1,0:T(4,128)S(1)} %copy-done.4, s32[8,128]{1,0:T(8,128)S(1)} %copy-done.2, s32[8,128]{1,0:T(8,128)S(1)} %copy-done.3, s32[128]{0:T(128)S(1)} %copy-done.5, ...), custom_call_target="tpu_custom_call" | custom-call | tf_op jit(solution)/shard_map/inversion/pallas_call | solution.py:329
  80.9 0.7 copy.11
  81.5 0.7 copy.12
Async XLA Ops:
  0.6 2.2 %copy-start = (bf16[8,512,512]{2,1,0:T(8,128)(2,1)S(1)}, bf16[8,512,512]{2,1,0:T(8,128)(2,1)}, u32[]{:S(2)}) copy-start(bf16[8,512,512]{2,1,0:T(8,128)(2,1)} %kernels_ref.1) | copy-start | bytes 12582916
  2.8 0.9 %copy-start.1 = (bf16[128,512]{1,0:T(8,128)(2,1)S(1)}, bf16[128,512]{1,0:T(8,128)(2,1)}, u32[]{:S(2)}) copy-start(bf16[128,512]{1,0:T(8,128)(2,1)} %traces_ref.1) | copy-start | bytes 393220
  3.7 0.7 copy-start.2
  4.4 0.7 copy-start.3
  5.1 0.7 copy-start.4
  5.8 0.7 copy-start.5
  6.4 0.7 copy-start.6

commit v2 on v1

--- a/solution.py
+++ b/solution.py
@@ -53,6 +53,12 @@
     solution_ref,
     residual_ref,
     moveout,
+    traces_in,
+    send_in,
+    slot_in,
+    pattern_in,
+    bin_in,
+    count_in,
     pick,
     spread_to,
     spread,
@@ -66,12 +72,10 @@
     smooth,
     edge_send,
     edge_land,
-    totals,
     total_send,
-    total_a,
-    total_b,
-    total_c,
+    total_land,
     load_sem,
+    table_sem,
     back_ssem,
     back_rsem,
     ahead_ssem,
@@ -82,24 +86,50 @@
     total_rsem,
 ):
     n_mid, n_off, n_z = sizes
-    n_y = n_mid // n_z
+    n_y, n_x = n_mid // n_z, n_off // 2
     samples = moveout.shape[2]
-    trace_rows = traces_ref.shape[0]
+    trace_rows = traces_in.shape[0]
     width = samples // CHUNKS
     mid = lax.axis_index("mid")
     off = lax.axis_index("off")
-    row_y = lax.div(mid, n_z)
-    col_z = lax.rem(mid, n_z)
+    row_y, col_z = lax.div(mid, n_z), lax.rem(mid, n_z)
+    col_x, core = lax.div(off, 2), lax.rem(off, 2)
 
     def tile_at(shift):
         return lax.rem(mid + (shift + n_mid), n_mid)
 
     tiles_to = [tile_at(s) for s in SHIFTS]
     tiles_back = [tile_at(-s) for s in SHIFTS]
-    off_peers = [lax.rem(off + d, n_off) for d in range(1, n_off)]
-    z_peers = [row_y * n_z + lax.rem(col_z + d, n_z) for d in range(1, n_z)]
-    y_peers = [lax.rem(row_y + d, n_y) * n_z + col_z for d in range(1, n_y)]
-
+
+    def farthest_first(sizes_2, where):
+        pairs = [(i, j) for i in range(sizes_2[0]) for j in range(sizes_2[1]) if i or j]
+        pairs.sort(key=lambda ij: -min(ij[0], sizes_2[0] - ij[0]) - min(ij[1], sizes_2[1] - ij[1]))
+        return [where(i, j) for i, j in pairs]
+
+    line = farthest_first(
+        (n_z, 2), lambda i, j: (row_y * n_z + lax.rem(col_z + i, n_z), col_x * 2 + lax.rem(core + j, 2))
+    )
+    plane = farthest_first(
+        (n_y, n_x),
+        lambda i, j: (lax.rem(row_y + i, n_y) * n_z + col_z, lax.rem(col_x + j, n_x) * 2 + core),
+    )
+    stages = (line, plane)
+
+    tables = [
+        pltpu.make_async_copy(src, dst, table_sem.at[i])
+        for i, (src, dst) in enumerate(
+            (
+                (slot_ref, slot_in),
+                (pattern_ref, pattern_in),
+                (bin_ref, bin_in),
+                (count_ref, count_in),
+                (send_ref, send_in),
+                (traces_ref, traces_in),
+            )
+        )
+    ]
+    for load in tables:
+        load.start()
     loads = [
         pltpu.make_async_copy(kernels_ref.at[p], moveout.at[p], load_sem.at[p]) for p in range(PATTERNS)
     ]
@@ -107,22 +137,22 @@
         load.start()
 
     barrier = pltpu.get_barrier_semaphore()
-    greeted = 0
-    for tile in tiles_to + z_peers + y_peers:
-        pl.semaphore_signal(barrier, inc=1, device_id=(tile, off), device_id_type=MESH)
-        greeted += 1
-    for peer in off_peers:
-        pl.semaphore_signal(barrier, inc=1, device_id=(mid, peer), device_id_type=MESH)
-        greeted += 1
-
-    slot = slot_ref[...]
-    live = lax.broadcasted_iota(jnp.int32, slot.shape, 0) < count_ref[...].reshape(1, trace_rows)
+    greeted = [device for stage in stages for device in stage]
+    greeted += [(tile, off) for tile in tiles_to]
+    greeted += [(mid, lax.rem(off + 1, n_off)), (mid, lax.rem(off + n_off - 1, n_off))]
+    for device in greeted:
+        pl.semaphore_signal(barrier, inc=1, device_id=device, device_id_type=MESH)
+    for load in tables:
+        load.wait()
+
+    slot = slot_in[...]
+    live = lax.broadcasted_iota(jnp.int32, slot.shape, 0) < count_in[...].reshape(1, trace_rows)
     for k in range(DIRS):
         source = mid - SHIFTS[k]
         here = (source >= 0) & (source < n_mid)
         inside = (slot >= CELLS + k * SEND) & (slot < CELLS + (k + 1) * SEND)
         live = live & (jnp.logical_not(inside) | here)
-    code = pattern_ref[...] * ROWS + slot * BINS + bin_ref[...].reshape(1, trace_rows)
+    code = pattern_in[...] * ROWS + slot * BINS + bin_in[...].reshape(1, trace_rows)
     code = jnp.where(live, code, -1)
     row_id = lax.broadcasted_iota(jnp.int32, (ROWS, trace_rows), 0)
     for p in range(PATTERNS):
@@ -136,7 +166,7 @@
     listed = jnp.zeros((OWN, AWAY), jnp.int32)
     for k in range(DIRS):
         for m in range(SEND):
-            listed = jnp.where(entry // BINS == k * SEND + m, send_ref[0, k, m], listed)
+            listed = jnp.where(entry // BINS == k * SEND + m, send_in[0, k : k + 1, m : m + 1], listed)
     place = listed * BINS + entry % BINS
     land_f32 = jnp.where(place == lax.broadcasted_iota(jnp.int32, (OWN, AWAY), 0), 1.0, 0.0)
     land_at = land_f32.astype(BF16)
@@ -190,7 +220,7 @@
         own[c] = sums[:OWN]
         back_send[turn, c] = sums[OWN:].astype(BF16)
         if first and c == 0:
-            pl.semaphore_wait(barrier, greeted)
+            pl.semaphore_wait(barrier, len(greeted))
         for k in FAR_FIRST:
             back_copy(turn, c, k).start()
 
@@ -231,81 +261,103 @@
                 out = out + dot(sums[p * trace_rows : (p + 1) * trace_rows], moveout[p, cols(c), :])
         return out
 
-    def total_copies(turn, stage):
-        land, where = stages[stage]
-        return [
+    def total_rows(turn, stage):
+        return total_land.at[turn, stage, pl.ds(0, len(stages[stage])), :]
+
+    def total_start(turn, stage, mine):
+        total_send[turn, stage, 0:1, :] = mine
+        for d, device in enumerate(stages[stage]):
             pltpu.make_async_remote_copy(
-                src_ref=total_send.at[turn, stage],
-                dst_ref=land.at[turn, d],
+                src_ref=total_send.at[turn, stage, pl.ds(0, 1), :],
+                dst_ref=total_land.at[turn, stage, pl.ds(d, 1), :],
                 send_sem=total_ssem.at[turn, stage],
                 recv_sem=total_rsem.at[turn, stage],
                 device_id=device,
                 device_id_type=MESH,
-            )
-            for d, device in enumerate(where)
-        ]
-
-    stages = [
-        (total_a, [(mid, peer) for peer in off_peers]),
-        (total_b, [(tile, off) for tile in z_peers]),
-        (total_c, [(tile, off) for tile in y_peers]),
-    ]
-
-    def total_start(turn, stage, mine):
-        total_send[turn, stage] = mine
-        for copy in total_copies(turn, stage):
-            copy.start()
+            ).start()
 
     def total_end(turn, stage):
-        land = stages[stage][0]
-        await_bytes(land.at[turn], total_rsem.at[turn, stage])
-        return total_send[turn, stage] + jnp.sum(land[turn], axis=0)
-
-    values = traces_ref[...]
+        await_bytes(total_rows(turn, stage), total_rsem.at[turn, stage])
+        heard = total_land[turn, stage, 0 : len(stages[stage]), :]
+        return total_send[turn, stage, 0:1, :] + jnp.sum(heard, axis=0, keepdims=True)
+
+    lane = lax.broadcasted_iota(jnp.int32, (1, 128), 1)
+
+    def packed(parts):
+        out = jnp.zeros((1, 128), F32)
+        for i, part in enumerate(parts):
+            part = part + pltpu.roll(part, 64, 1)
+            part = part + pltpu.roll(part, 32, 1)
+            out = jnp.where(lane // 32 == i, part, out)
+        return out
+
+    def unpacked(row, i):
+        return jnp.sum(jnp.where(lane // 32 == i, row, 0.0), axis=1, keepdims=True)
+
+    values = traces_in[...]
     for c in range(CHUNKS):
         adjoint_chunk(0, c, values, first=True)
+    heard = values.astype(F32)
+    power = by_lanes(heard * heard)
     norm = jnp.zeros((1, 128), F32)
     for c in range(CHUNKS):
         part = landed(0, c)
         ahead_chunk(0, c, part)
         field0[:, cols(c)] = part
         norm = norm + by_lanes(part * part)
-
-    for turn, field in ((0, field0), (1, field1)):
-        send_edges(turn, field)
-        smooth[...] = smoothed(turn, field)
-        cross = by_lanes(field[...] * smooth[...])
-        values = forward(turn).astype(BF16)
-        heard = values.astype(F32)
-        totals[0:1, :] = norm
-        totals[1:2, :] = by_lanes(heard * heard) + cross
-        totals[2:8, :] = jnp.zeros((6, 128), F32)
-        total_start(turn, 0, totals[...])
-        for c in range(CHUNKS):
-            adjoint_chunk(turn + 1, c, values)
-            if c < 2:
-                total_start(turn, c + 1, total_end(turn, c))
-        sums = jnp.sum(total_end(turn, 2), axis=1, keepdims=True)
-        if turn == 0:
-            norm_0 = sums[0:1, :]
-            step_0 = norm_0 / sums[1:2, :]
-            norm = jnp.zeros((1, 128), F32)
-            for c in range(CHUNKS):
-                part = field0[:, cols(c)] - step_0 * (landed(1, c) + smooth[:, cols(c)])
-                ahead_chunk(1, c, part)
-                field1[:, cols(c)] = part
-                norm = norm + by_lanes(part * part)
-        else:
-            norm_1 = sums[0:1, :]
-            ratio = norm_1 / norm_0
-            step_1 = norm_1 / (sums[1:2, :] - ratio * (norm_1 / step_0))
-            older = step_1 * ratio
-            for c in range(CHUNKS):
-                r, q = field0[:, cols(c)], field1[:, cols(c)]
-                image = landed(2, c) + smooth[:, cols(c)]
-                cube = (CELLS, BINS, width)
-                solution_ref[:, :, cols(c)] = ((step_0 + older) * r + step_1 * q).reshape(cube)
-                residual_ref[:, :, cols(c)] = (q - step_1 * image - (older / step_0) * (r - q)).reshape(cube)
+    total_start(0, 0, packed((power, norm)))
+
+    send_edges(0, field0)
+    smooth[...] = smoothed(0, field0)
+    cross = by_lanes(field0[...] * smooth[...])
+    values = forward(0).astype(BF16)
+    heard = values.astype(F32)
+    curve_r = by_lanes(heard * heard) + cross
+    adjoint_chunk(1, 0, values)
+    total_start(0, 1, total_end(0, 0))
+    for c in range(1, CHUNKS):
+        adjoint_chunk(1, c, values)
+    sums = total_end(0, 1)
+    power, rr = unpacked(sums, 0), unpacked(sums, 1)
+    usual = jnp.maximum(2.0 * rr / power, 1.0 / 128.0)
+    slope = 1.5 * (usual + jnp.minimum(usual, 2.0 * smooth_weight))
+    guess = 1.0 / slope
+    norm = jnp.zeros((1, 128), F32)
+    for c in range(CHUNKS):
+        part = field0[:, cols(c)] - guess * (landed(1, c) + smooth[:, cols(c)])
+        ahead_chunk(1, c, part)
+        field1[:, cols(c)] = part
+        norm = norm + by_lanes(part * part)
+
+    send_edges(1, field1)
+    smooth[...] = smoothed(1, field1)
+    cross = by_lanes(field1[...] * smooth[...])
+    values = forward(1).astype(BF16)
+    heard = values.astype(F32)
+    total_start(1, 0, packed((curve_r, norm, by_lanes(heard * heard) + cross)))
+    for c in range(CHUNKS):
+        adjoint_chunk(2, c, values)
+    total_start(1, 1, total_end(1, 0))
+    for c in range(CHUNKS):
+        smooth[:, cols(c)] = landed(2, c) + smooth[:, cols(c)]
+    sums = total_end(1, 1)
+    ra, zz, za = (unpacked(sums, i) for i in range(3))
+
+    step_0 = rr / ra
+    t = step_0 * slope
+    rest = 1.0 - t
+    rz = rr - guess * ra
+    norm_1 = rest * (rest * rr + 2.0 * t * rz) + t * (t * zz)
+    curve_1 = rest * (rest * ra + 2.0 * t * ((rz - zz) * slope)) + t * (t * za)
+    ratio = norm_1 / rr
+    step_1 = norm_1 / (curve_1 - ratio * (norm_1 / step_0))
+    for c in range(CHUNKS):
+        r, z = field0[:, cols(c)], field1[:, cols(c)]
+        cube = (CELLS, BINS, width)
+        solution_ref[:, :, cols(c)] = ((step_0 + step_1 * (ratio + rest)) * r + (step_1 * t) * z).reshape(cube)
+        residual_ref[:, :, cols(c)] = (
+            rest * r + t * z - (step_1 * (ratio + rest) * slope) * (r - z) - (step_1 * t) * smooth[:, cols(c)]
+        ).reshape(cube)
 
     for turn in range(3):
         for c in range(CHUNKS):
@@ -315,8 +367,8 @@
             await_bytes(ahead_send.at[turn, c], ahead_ssem.at[turn, c])
         for side in range(2):
             await_bytes(edge_send.at[turn, side], edge_ssem.at[turn, side])
-        for stage in range(3):
-            await_bytes(stages[stage][0].at[turn], total_ssem.at[turn, stage])
+        for stage in range(2):
+            await_bytes(total_rows(turn, stage), total_ssem.at[turn, stage])
 
 
 def shards(sizes, traces, kernels, send_list, aper_slot, aper_pattern, trace_bin, trace_count):
@@ -325,22 +377,21 @@
     trace_rows, samples = traces.shape
     width = samples // CHUNKS
     vmem = pl.BlockSpec(memory_space=pltpu.VMEM)
+    hbm = pl.BlockSpec(memory_space=pltpu.HBM)
     shape = jax.ShapeDtypeStruct((CELLS, BINS, samples), F32)
     return pl.pallas_call(
         functools.partial(body, sizes),
         out_shape=(shape, shape),
-        in_specs=[
-            vmem,
-            pl.BlockSpec(memory_space=pl.ANY),
-            pl.BlockSpec(memory_space=pltpu.SMEM),
-            vmem,
-            vmem,
-            vmem,
-            vmem,
-        ],
+        in_specs=[hbm] * 7,
         out_specs=(vmem, vmem),
         scratch_shapes=[
             pltpu.VMEM((PATTERNS, samples, samples), BF16),
+            pltpu.VMEM((trace_rows, samples), BF16),
+            pltpu.VMEM(send_list.shape, jnp.int32),
+            pltpu.VMEM((APER, trace_rows), jnp.int32),
+            pltpu.VMEM((APER, trace_rows), jnp.int32),
+            pltpu.VMEM((trace_rows,), jnp.int32),
+            pltpu.VMEM((trace_rows,), jnp.int32),
             pltpu.VMEM((PATTERNS * trace_rows, ROWS), BF16),
             pltpu.VMEM((ROWS, PATTERNS * trace_rows), BF16),
             pltpu.VMEM((PATTERNS * trace_rows, width), BF16),
@@ -354,23 +405,21 @@
             pltpu.VMEM((OWN, samples), F32),
             pltpu.VMEM((2, 2, CELLS, samples), F32),
             pltpu.VMEM((2, 2, CELLS, samples), F32),
-            pltpu.VMEM((8, 128), F32),
-            pltpu.VMEM((2, 3, 8, 128), F32),
-            pltpu.VMEM((2, n_off - 1, 8, 128), F32),
-            pltpu.VMEM((2, n_z - 1, 8, 128), F32),
-            pltpu.VMEM((2, n_y - 1, 8, 128), F32),
+            pltpu.VMEM((2, 2, 8, 128), F32),
+            pltpu.VMEM((2, 2, max(n_z * 2, n_y * n_off // 2), 128), F32),
             pltpu.SemaphoreType.DMA((PATTERNS,)),
+            pltpu.SemaphoreType.DMA((6,)),
             pltpu.SemaphoreType.DMA((3, CHUNKS)),
             pltpu.SemaphoreType.DMA((3, CHUNKS)),
             pltpu.SemaphoreType.DMA((2, CHUNKS)),
             pltpu.SemaphoreType.DMA((2, CHUNKS)),
             pltpu.SemaphoreType.DMA((2, 2)),
             pltpu.SemaphoreType.DMA((2, 2)),
-            pltpu.SemaphoreType.DMA((2, 3)),
-            pltpu.SemaphoreType.DMA((2, 3)),
+            pltpu.SemaphoreType.DMA((2, 2)),
+            pltpu.SemaphoreType.DMA((2, 2)),
         ],
         compiler_params=pltpu.CompilerParams(
-            collective_id=0, has_side_effects=True, vmem_limit_bytes=40 * 2**20
+            collective_id=0, has_side_effects=True, vmem_limit_bytes=60 * 2**20
         ),
         name="inversion",
     )(traces, kernels, send_list, aper_slot, aper_pattern, trace_bin, trace_count)

time: 82.5 us -> 66.1 us (0.80)
  the two profiles are of different devices: /device:TPU:2 before, /device:TPU:1 now
where the time goes in v2:
time: 66.1 us; the launch traced here: 65.9 us
  Pallas kernels  62.1 us (94%)
  local copies, waits for them, and re-layouts  3.14 us (5%)
    pallas_call x1, Pallas kernels, shards(): pl.pallas_call(functools.partial(body, sizes), out_shape=(shape, shape),...  62.1 us
    unnamed x2, local copies, waits for them, and re-layouts  3.14 us

profile of v2, /device:TPU:1, one launch (start us, length us, event | category | flops | bytes accessed | tf_op | source)
XLA Modules:
  0.0 65.9 jit_solution(17797062748961999338)
XLA Ops:
  0.6 62.1 %inversion.1 = (f32[8,8,512]{2,1,0:T(8,128)}, f32[8,8,512]{2,1,0:T(8,128)}) custom-call(bf16[128,512]{1,0:T(8,128)(2,1)} %traces_ref.1, bf16[8,512,512]{2,1,0:T(8,128)(2,1)} %kernels_ref.1, s32[1,4,4]{2,1,0:T(4,128)} %send_ref.1, s32[8,128]{1,0:T(8,128)} %slot_ref.1, s32[8,128]{1,0:T(8,128)} %pattern_ref.1, s32[128]{0:T(128)} %bin_ref.1, s32[128]{0:T(128)} %count_ref.1), custom_call_target="tpu_custom_call" | custom-call | tf_op jit(solution)/shard_map/inversion/pallas_call | solution.py:382
  62.8 1.6 %copy.11 = f32[8,8,512]{2,1,0:T(8,128)} copy(f32[8,8,512]{2,1,0:T(8,128)} %get-tuple-element.4) | data formatting | bytes 262144
  64.3 1.6 %copy.12 = f32[8,8,512]{2,1,0:T(8,128)} copy(f32[8,8,512]{2,1,0:T(8,128)} %get-tuple-element.5) | data formatting | bytes 262144

commit v3 on v2

--- a/solution.py
+++ b/solution.py
@@ -50,8 +50,10 @@
     pattern_ref,
     bin_ref,
     count_ref,
-    solution_ref,
-    residual_ref,
+    first_ref,
+    second_ref,
+    image_ref,
+    weights_ref,
     moveout,
     traces_in,
     send_in,
@@ -59,6 +61,7 @@
     pattern_in,
     bin_in,
     count_in,
+    turned,
     pick,
     spread_to,
     spread,
@@ -76,6 +79,7 @@
     total_land,
     load_sem,
     table_sem,
+    store_sem,
     back_ssem,
     back_rsem,
     ahead_ssem,
@@ -113,7 +117,7 @@
         (n_y, n_x),
         lambda i, j: (lax.rem(row_y + i, n_y) * n_z + col_z, lax.rem(col_x + j, n_x) * 2 + core),
     )
-    stages = (line, plane)
+    stages = (plane, line)
 
     tables = [
         pltpu.make_async_copy(src, dst, table_sem.at[i])
@@ -211,11 +215,20 @@
         pltpu.make_async_copy(ref, ref, sem).wait()
 
     def adjoint_chunk(turn, c, values, first=False):
-        for p in range(PATTERNS):
-            if first and c == 0:
-                loads[p].wait()
-            part = dot_t(values, moveout[p, cols(c), :])
-            spread[p * trace_rows : (p + 1) * trace_rows, :] = part.astype(BF16)
+        groups = 2 if first else 1
+        each = PATTERNS // groups
+        for g in range(groups):
+            if first:
+                if c == 0:
+                    for load in loads[g * each : (g + 1) * each]:
+                        load.wait()
+                wide = dot_t(values, moveout[g * each : (g + 1) * each, cols(c), :].reshape(each * width, samples))
+            else:
+                wide = dot(values, turned[c])
+            wide = wide.astype(BF16)
+            for i in range(each):
+                p = g * each + i
+                spread[p * trace_rows : (p + 1) * trace_rows, :] = wide[:, i * width : (i + 1) * width]
         sums = dot(spread_to[...], spread[...])
         own[c] = sums[:OWN]
         back_send[turn, c] = sums[OWN:].astype(BF16)
@@ -223,17 +236,19 @@
             pl.semaphore_wait(barrier, len(greeted))
         for k in FAR_FIRST:
             back_copy(turn, c, k).start()
+        return sums
 
     def landed(turn, c):
         await_bytes(back_land.at[turn, c], back_rsem.at[turn, c])
         return own[c] + dot(land_at, back_land[turn, c])
 
-    def ahead_chunk(turn, c, part):
+    def ahead_chunk(turn, c, part, field):
         rounded = part.astype(BF16)
         ahead_send[turn, c] = dot(take_from, rounded).astype(BF16)
         for k in FAR_FIRST:
             ahead_copy(turn, c, k).start()
         slots[turn, c, :OWN, :] = rounded
+        field[:, cols(c)] = part
 
     def send_edges(turn, field):
         cube = field[...].reshape(CELLS, BINS, samples)
@@ -253,12 +268,13 @@
         return out.reshape(OWN, samples)
 
     def forward(turn):
-        out = jnp.zeros((trace_rows, samples), F32)
+        out = None
         for c in range(CHUNKS):
             await_bytes(slots.at[turn, c, pl.ds(OWN, AWAY), :], ahead_rsem.at[turn, c])
             sums = dot(pick[...], slots[turn, c]).astype(BF16)
-            for p in range(PATTERNS):
-                out = out + dot(sums[p * trace_rows : (p + 1) * trace_rows], moveout[p, cols(c), :])
+            wide = jnp.concatenate([sums[p * trace_rows : (p + 1) * trace_rows] for p in range(PATTERNS)], axis=1)
+            part = dot(wide, moveout[:, cols(c), :].reshape(PATTERNS * width, samples))
+            out = part if out is None else out + part
         return out
 
     def total_rows(turn, stage):
@@ -294,54 +310,63 @@
     def unpacked(row, i):
         return jnp.sum(jnp.where(lane // 32 == i, row, 0.0), axis=1, keepdims=True)
 
+    stores = [
+        pltpu.make_async_copy(src, dst, store_sem.at[i])
+        for i, (src, dst) in enumerate(((field0, first_ref), (field1, second_ref), (smooth, image_ref)))
+    ]
+
     values = traces_in[...]
-    for c in range(CHUNKS):
-        adjoint_chunk(0, c, values, first=True)
+    local = jnp.zeros((1, 128), F32)
+    for c in range(CHUNKS):
+        part = adjoint_chunk(0, c, values, first=True)
+        local = local + by_lanes(part * part)
     heard = values.astype(F32)
-    power = by_lanes(heard * heard)
+    total_start(0, 0, packed((by_lanes(heard * heard), local)))
+    for c in range(CHUNKS):
+        for p in range(PATTERNS):
+            turned[c, :, p * width : (p + 1) * width] = moveout[p, cols(c), :].T
     norm = jnp.zeros((1, 128), F32)
     for c in range(CHUNKS):
         part = landed(0, c)
-        ahead_chunk(0, c, part)
-        field0[:, cols(c)] = part
+        ahead_chunk(0, c, part, field0)
         norm = norm + by_lanes(part * part)
-    total_start(0, 0, packed((power, norm)))
+    norm_r = norm
 
     send_edges(0, field0)
+    stores[0].start()
+    total_start(0, 1, total_end(0, 0))
     smooth[...] = smoothed(0, field0)
     cross = by_lanes(field0[...] * smooth[...])
     values = forward(0).astype(BF16)
     heard = values.astype(F32)
     curve_r = by_lanes(heard * heard) + cross
-    adjoint_chunk(1, 0, values)
-    total_start(0, 1, total_end(0, 0))
-    for c in range(1, CHUNKS):
+    for c in range(CHUNKS):
         adjoint_chunk(1, c, values)
     sums = total_end(0, 1)
-    power, rr = unpacked(sums, 0), unpacked(sums, 1)
-    usual = jnp.maximum(2.0 * rr / power, 1.0 / 128.0)
+    usual = jnp.maximum(2.0 * unpacked(sums, 1) / unpacked(sums, 0), 1.0 / 128.0)
     slope = 1.5 * (usual + jnp.minimum(usual, 2.0 * smooth_weight))
     guess = 1.0 / slope
     norm = jnp.zeros((1, 128), F32)
     for c in range(CHUNKS):
         part = field0[:, cols(c)] - guess * (landed(1, c) + smooth[:, cols(c)])
-        ahead_chunk(1, c, part)
-        field1[:, cols(c)] = part
+        ahead_chunk(1, c, part, field1)
         norm = norm + by_lanes(part * part)
 
     send_edges(1, field1)
+    stores[1].start()
     smooth[...] = smoothed(1, field1)
     cross = by_lanes(field1[...] * smooth[...])
     values = forward(1).astype(BF16)
     heard = values.astype(F32)
-    total_start(1, 0, packed((curve_r, norm, by_lanes(heard * heard) + cross)))
+    total_start(1, 0, packed((curve_r, norm, norm_r, by_lanes(heard * heard) + cross)))
     for c in range(CHUNKS):
         adjoint_chunk(2, c, values)
     total_start(1, 1, total_end(1, 0))
     for c in range(CHUNKS):
         smooth[:, cols(c)] = landed(2, c) + smooth[:, cols(c)]
+    stores[2].start()
     sums = total_end(1, 1)
-    ra, zz, za = (unpacked(sums, i) for i in range(3))
+    ra, zz, rr, za = (unpacked(sums, i) for i in range(4))
 
     step_0 = rr / ra
     t = step_0 * slope
@@ -351,13 +376,16 @@
     curve_1 = rest * (rest * ra + 2.0 * t * ((rz - zz) * slope)) + t * (t * za)
     ratio = norm_1 / rr
     step_1 = norm_1 / (curve_1 - ratio * (norm_1 / step_0))
-    for c in range(CHUNKS):
-        r, z = field0[:, cols(c)], field1[:, cols(c)]
-        cube = (CELLS, BINS, width)
-        solution_ref[:, :, cols(c)] = ((step_0 + step_1 * (ratio + rest)) * r + (step_1 * t) * z).reshape(cube)
-        residual_ref[:, :, cols(c)] = (
-            rest * r + t * z - (step_1 * (ratio + rest) * slope) * (r - z) - (step_1 * t) * smooth[:, cols(c)]
-        ).reshape(cube)
+    along = step_1 * (ratio + rest)
+    row = lax.broadcasted_iota(jnp.int32, (8, 128), 0)
+    weights = jnp.zeros((8, 128), F32)
+    for i, weight in enumerate(
+        (step_0 + along, step_1 * t, rest - along * slope, t + along * slope, -(step_1 * t))
+    ):
+        weights = jnp.where(row == i, weight, weights)
+    weights_ref[...] = weights
+    for store in stores:
+        store.wait()
 
     for turn in range(3):
         for c in range(CHUNKS):
@@ -371,6 +399,14 @@
             await_bytes(total_rows(turn, stage), total_ssem.at[turn, stage])
 
 
+def combine(r_ref, z_ref, image_ref, weights_ref, solution_ref, residual_ref):
+    weight = [weights_ref[i : i + 1, 0:1] for i in range(5)]
+    r, z = r_ref[...], z_ref[...]
+    solution_ref[...] = (weight[0] * r + weight[1] * z).reshape(solution_ref.shape)
+    left = weight[2] * r + weight[3] * z + weight[4] * image_ref[...]
+    residual_ref[...] = left.reshape(residual_ref.shape)
+
+
 def shards(sizes, traces, kernels, send_list, aper_slot, aper_pattern, trace_bin, trace_count):
     n_mid, n_off, n_z = sizes
     n_y = n_mid // n_z
@@ -378,12 +414,12 @@
     width = samples // CHUNKS
     vmem = pl.BlockSpec(memory_space=pltpu.VMEM)
     hbm = pl.BlockSpec(memory_space=pltpu.HBM)
-    shape = jax.ShapeDtypeStruct((CELLS, BINS, samples), F32)
-    return pl.pallas_call(
+    field = jax.ShapeDtypeStruct((OWN, samples), F32)
+    r, z, image, weights = pl.pallas_call(
         functools.partial(body, sizes),
-        out_shape=(shape, shape),
+        out_shape=(field, field, field, jax.ShapeDtypeStruct((8, 128), F32)),
         in_specs=[hbm] * 7,
-        out_specs=(vmem, vmem),
+        out_specs=(hbm, hbm, hbm, vmem),
         scratch_shapes=[
             pltpu.VMEM((PATTERNS, samples, samples), BF16),
             pltpu.VMEM((trace_rows, samples), BF16),
@@ -392,6 +428,7 @@
             pltpu.VMEM((APER, trace_rows), jnp.int32),
             pltpu.VMEM((trace_rows,), jnp.int32),
             pltpu.VMEM((trace_rows,), jnp.int32),
+            pltpu.VMEM((CHUNKS, samples, PATTERNS * width), BF16),
             pltpu.VMEM((PATTERNS * trace_rows, ROWS), BF16),
             pltpu.VMEM((ROWS, PATTERNS * trace_rows), BF16),
             pltpu.VMEM((PATTERNS * trace_rows, width), BF16),
@@ -409,6 +446,7 @@
             pltpu.VMEM((2, 2, max(n_z * 2, n_y * n_off // 2), 128), F32),
             pltpu.SemaphoreType.DMA((PATTERNS,)),
             pltpu.SemaphoreType.DMA((6,)),
+            pltpu.SemaphoreType.DMA((3,)),
             pltpu.SemaphoreType.DMA((3, CHUNKS)),
             pltpu.SemaphoreType.DMA((3, CHUNKS)),
             pltpu.SemaphoreType.DMA((2, CHUNKS)),
@@ -423,6 +461,15 @@
         ),
         name="inversion",
     )(traces, kernels, send_list, aper_slot, aper_pattern, trace_bin, trace_count)
+    shape = jax.ShapeDtypeStruct((CELLS, BINS, samples), F32)
+    return pl.pallas_call(
+        combine,
+        out_shape=(shape, shape),
+        in_specs=[vmem] * 4,
+        out_specs=(vmem, vmem),
+        compiler_params=pltpu.CompilerParams(vmem_limit_bytes=60 * 2**20),
+        name="combine",
+    )(r, z, image, weights)
 
 
 def solution(mesh):

time: 66.1 us -> 62.7 us (0.949)
  local copies, waits for them, and re-layouts: 3.14 us -> 0 us
    unnamed x2 -> x0, local copies, waits for them, and re-layouts: 3.14 us -> none
    pallas_call x1 -> x2, Pallas kernels: 62.1 us -> 61.9 us  [the longest x1 60.1 us: shards(): pl.pallas_call(functools.partial(body, sizes), out_shape=(field, field, f...]
where the time goes in v3:
time: 62.7 us; the launch traced here: 62.5 us
  Pallas kernels  61.9 us (99%)
  between operations  0.64 us (1%)
    pallas_call x1, Pallas kernels, shards(): pl.pallas_call(functools.partial(body, sizes), out_shape=(field, field, f...  60.1 us
    pallas_call x1, Pallas kernels, shards(): pl.pallas_call(combine, out_shape=(shape, shape), in_specs=[vmem] * 4, ou...  1.79 us

profile of v3, /device:TPU:1, one launch (start us, length us, event | category | flops | bytes accessed | tf_op | source)
XLA Modules:
  0.0 62.5 jit_solution(13776177684506537328)
XLA Ops:
  0.6 60.1 %inversion.1 = (f32[64,512]{1,0:T(8,128)}, f32[64,512]{1,0:T(8,128)}, f32[64,512]{1,0:T(8,128)}, f32[8,128]{1,0:T(8,128)}) custom-call(bf16[128,512]{1,0:T(8,128)(2,1)} %traces_ref.1, bf16[8,512,512]{2,1,0:T(8,128)(2,1)} %kernels_ref.1, s32[1,4,4]{2,1,0:T(4,128)} %send_ref.1, s32[8,128]{1,0:T(8,128)} %slot_ref.1, s32[8,128]{1,0:T(8,128)} %pattern_ref.1, ...), custom_call_target="tpu_custom_call" | custom-call | tf_op jit(solution)/shard_map/inversion/pallas_call | solution.py:418
  60.7 1.8 %combine.1 = (f32[8,8,512]{2,1,0:T(8,128)}, f32[8,8,512]{2,1,0:T(8,128)}) custom-call(f32[64,512]{1,0:T(8,128)} %get-tuple-element.6.r_ref, f32[64,512]{1,0:T(8,128)} %get-tuple-element.7.z_ref, f32[64,512]{1,0:T(8,128)} %get-tuple-element.8.image_ref, f32[8,128]{1,0:T(8,128)} %get-tuple-element.9.weights_ref), custom_call_target="tpu_custom_call" | custom-call | tf_op jit(solution)/shard_map/combine/pallas_call | solution.py:465

commit v4 on v3

--- a/solution.py
+++ b/solution.py
@@ -21,6 +21,7 @@
 CHUNKS = 2
 SHIFTS = (1, -1, 2, -2)
 FAR_FIRST = (2, 3, 0, 1)
+SHRINK = 2.0 ** -14
 smooth_weight = 2.0
 F32 = jnp.float32
 BF16 = jnp.bfloat16
@@ -65,9 +66,12 @@
     pick,
     spread_to,
     spread,
+    spread_low,
     own,
     back_send,
     back_land,
+    fine_send,
+    fine_land,
     slots,
     ahead_send,
     field0,
@@ -88,6 +92,7 @@
     edge_rsem,
     total_ssem,
     total_rsem,
+    meet_sem,
 ):
     n_mid, n_off, n_z = sizes
     n_y, n_x = n_mid // n_z, n_off // 2
@@ -132,20 +137,45 @@
             )
         )
     ]
-    for load in tables:
-        load.start()
     loads = [
         pltpu.make_async_copy(kernels_ref.at[p], moveout.at[p], load_sem.at[p]) for p in range(PATTERNS)
     ]
-    for load in loads:
+
+    barrier = pltpu.get_barrier_semaphore()
+
+    def greet(devices):
+        for device in devices:
+            pl.semaphore_signal(barrier, inc=1, device_id=device, device_id_type=MESH)
+
+    def around(count, steps):
+        return sorted({d % count for step in steps for d in (step, -step)} - {0})
+
+    def at_z(steps):
+        return [(row_y * n_z + lax.rem(col_z + d, n_z), off) for d in around(n_z, steps)]
+
+    def at_y(steps):
+        return [(lax.rem(row_y + d, n_y) * n_z + col_z, off) for d in around(n_y, steps)]
+
+    def at_x(steps):
+        return [(mid, lax.rem(col_x + d, n_x) * 2 + core) for d in around(n_x, steps)]
+
+    partner = [(mid, col_x * 2 + 1 - core)]
+    near = [(tile, off) for tile in tiles_to]
+    near += [(mid, lax.rem(off + 1, n_off)), (mid, lax.rem(off + n_off - 1, n_off))]
+    near += at_z((1, 2)) + at_y((1,)) + at_x((1,)) + partner
+    rounds = (at_z((2,)) + at_y((1,)) + at_x((1,)), at_z((4,)) + at_y((2,)), at_x((1, 2)) + partner)
+
+    def meet(i):
+        for device in rounds[i]:
+            pl.semaphore_signal(meet_sem.at[i], inc=1, device_id=device, device_id_type=MESH)
+
+    def met(i):
+        if rounds[i]:
+            pl.semaphore_wait(meet_sem.at[i], len(rounds[i]))
+
+    greet(near)
+    for load in tables + loads:
         load.start()
-
-    barrier = pltpu.get_barrier_semaphore()
-    greeted = [device for stage in stages for device in stage]
-    greeted += [(tile, off) for tile in tiles_to]
-    greeted += [(mid, lax.rem(off + 1, n_off)), (mid, lax.rem(off + n_off - 1, n_off))]
-    for device in greeted:
-        pl.semaphore_signal(barrier, inc=1, device_id=device, device_id_type=MESH)
     for load in tables:
         load.wait()
 
@@ -233,10 +263,43 @@
         own[c] = sums[:OWN]
         back_send[turn, c] = sums[OWN:].astype(BF16)
         if first and c == 0:
-            pl.semaphore_wait(barrier, len(greeted))
+            pl.semaphore_wait(barrier, len(near))
         for k in FAR_FIRST:
             back_copy(turn, c, k).start()
         return sums
+
+    def halves(x):
+        high = x.astype(BF16)
+        return high, (x - high.astype(F32)).astype(BF16)
+
+    def fine_copy(c, k):
+        part = pl.ds(k * PART, PART)
+        return pltpu.make_async_remote_copy(
+            src_ref=fine_send.at[c, part, :],
+            dst_ref=fine_land.at[c, part, :],
+            send_sem=back_ssem.at[2, c],
+            recv_sem=back_rsem.at[2, c],
+            device_id=(tiles_back[k], off),
+            device_id_type=MESH,
+        )
+
+    def fine_chunk(c, values):
+        high, low = halves(values)
+        wide = halves(dot(high, turned[c]) + dot(low, turned[c]))
+        for p in range(PATTERNS):
+            rows = slice(p * trace_rows, (p + 1) * trace_rows)
+            for part, to in zip(wide, (spread, spread_low)):
+                to[rows, :] = part[:, p * width : (p + 1) * width]
+        sums = dot(spread_to[...], spread[...]) + dot(spread_to[...], spread_low[...])
+        own[c] = sums[:OWN]
+        fine_send[c] = sums[OWN:]
+        for k in FAR_FIRST:
+            fine_copy(c, k).start()
+
+    def fine_landed(c):
+        await_bytes(fine_land.at[c], back_rsem.at[2, c])
+        high, low = halves(fine_land[c])
+        return own[c] + (dot(land_at, high) + dot(land_at, low))
 
     def landed(turn, c):
         await_bytes(back_land.at[turn, c], back_rsem.at[turn, c])
@@ -316,15 +379,14 @@
     ]
 
     values = traces_in[...]
-    local = jnp.zeros((1, 128), F32)
-    for c in range(CHUNKS):
-        part = adjoint_chunk(0, c, values, first=True)
-        local = local + by_lanes(part * part)
-    heard = values.astype(F32)
-    total_start(0, 0, packed((by_lanes(heard * heard), local)))
+    for c in range(CHUNKS):
+        adjoint_chunk(0, c, values, first=True)
+    meet(0)
     for c in range(CHUNKS):
         for p in range(PATTERNS):
             turned[c, :, p * width : (p + 1) * width] = moveout[p, cols(c), :].T
+    met(0)
+    meet(1)
     norm = jnp.zeros((1, 128), F32)
     for c in range(CHUNKS):
         part = landed(0, c)
@@ -334,21 +396,18 @@
 
     send_edges(0, field0)
     stores[0].start()
-    total_start(0, 1, total_end(0, 0))
     smooth[...] = smoothed(0, field0)
     cross = by_lanes(field0[...] * smooth[...])
+    met(1)
+    meet(2)
     values = forward(0).astype(BF16)
     heard = values.astype(F32)
     curve_r = by_lanes(heard * heard) + cross
     for c in range(CHUNKS):
         adjoint_chunk(1, c, values)
-    sums = total_end(0, 1)
-    usual = jnp.maximum(2.0 * unpacked(sums, 1) / unpacked(sums, 0), 1.0 / 128.0)
-    slope = 1.5 * (usual + jnp.minimum(usual, 2.0 * smooth_weight))
-    guess = 1.0 / slope
     norm = jnp.zeros((1, 128), F32)
     for c in range(CHUNKS):
-        part = field0[:, cols(c)] - guess * (landed(1, c) + smooth[:, cols(c)])
+        part = (landed(1, c) + smooth[:, cols(c)]) * SHRINK
         ahead_chunk(1, c, part, field1)
         norm = norm + by_lanes(part * part)
 
@@ -356,47 +415,46 @@
     stores[1].start()
     smooth[...] = smoothed(1, field1)
     cross = by_lanes(field1[...] * smooth[...])
-    values = forward(1).astype(BF16)
-    heard = values.astype(F32)
+    met(2)
+    heard = forward(1)
     total_start(1, 0, packed((curve_r, norm, norm_r, by_lanes(heard * heard) + cross)))
     for c in range(CHUNKS):
-        adjoint_chunk(2, c, values)
+        fine_chunk(c, heard)
     total_start(1, 1, total_end(1, 0))
     for c in range(CHUNKS):
-        smooth[:, cols(c)] = landed(2, c) + smooth[:, cols(c)]
+        smooth[:, cols(c)] = fine_landed(c) + smooth[:, cols(c)]
     stores[2].start()
     sums = total_end(1, 1)
     ra, zz, rr, za = (unpacked(sums, i) for i in range(4))
 
-    step_0 = rr / ra
-    t = step_0 * slope
-    rest = 1.0 - t
-    rz = rr - guess * ra
-    norm_1 = rest * (rest * rr + 2.0 * t * rz) + t * (t * zz)
-    curve_1 = rest * (rest * ra + 2.0 * t * ((rz - zz) * slope)) + t * (t * za)
-    ratio = norm_1 / rr
-    step_1 = norm_1 / (curve_1 - ratio * (norm_1 / step_0))
-    along = step_1 * (ratio + rest)
+    grow = 1.0 / SHRINK
+    step_0, one_over = rr / ra, 1.0 / rr
+    scaled = step_0 * grow
+    norm_1 = scaled * (scaled * zz) - rr
+    more = 1.0 + norm_1 * one_over
+    curve_1 = more * (more * ra) - 2.0 * more * (scaled * (zz * grow)) + scaled * (scaled * za)
+    step_1 = norm_1 / curve_1
+    along = step_1 * more
     row = lax.broadcasted_iota(jnp.int32, (8, 128), 0)
     weights = jnp.zeros((8, 128), F32)
     for i, weight in enumerate(
-        (step_0 + along, step_1 * t, rest - along * slope, t + along * slope, -(step_1 * t))
+        (step_0 + along, -(step_1 * scaled), jnp.ones_like(rr), -(scaled + along * grow), step_1 * scaled)
     ):
         weights = jnp.where(row == i, weight, weights)
     weights_ref[...] = weights
     for store in stores:
         store.wait()
 
-    for turn in range(3):
-        for c in range(CHUNKS):
+    for c in range(CHUNKS):
+        for turn in range(2):
             await_bytes(back_send.at[turn, c], back_ssem.at[turn, c])
+            await_bytes(ahead_send.at[turn, c], ahead_ssem.at[turn, c])
+        await_bytes(fine_send.at[c], back_ssem.at[2, c])
     for turn in range(2):
-        for c in range(CHUNKS):
-            await_bytes(ahead_send.at[turn, c], ahead_ssem.at[turn, c])
         for side in range(2):
             await_bytes(edge_send.at[turn, side], edge_ssem.at[turn, side])
-        for stage in range(2):
-            await_bytes(total_rows(turn, stage), total_ssem.at[turn, stage])
+    for stage in range(2):
+        await_bytes(total_rows(1, stage), total_ssem.at[1, stage])
 
 
 def combine(r_ref, z_ref, image_ref, weights_ref, solution_ref, residual_ref):
@@ -432,9 +490,12 @@
             pltpu.VMEM((PATTERNS * trace_rows, ROWS), BF16),
             pltpu.VMEM((ROWS, PATTERNS * trace_rows), BF16),
             pltpu.VMEM((PATTERNS * trace_rows, width), BF16),
+            pltpu.VMEM((PATTERNS * trace_rows, width), BF16),
             pltpu.VMEM((CHUNKS, OWN, width), F32),
-            pltpu.VMEM((3, CHUNKS, AWAY, width), BF16),
-            pltpu.VMEM((3, CHUNKS, AWAY, width), BF16),
+            pltpu.VMEM((2, CHUNKS, AWAY, width), BF16),
+            pltpu.VMEM((2, CHUNKS, AWAY, width), BF16),
+            pltpu.VMEM((CHUNKS, AWAY, width), F32),
+            pltpu.VMEM((CHUNKS, AWAY, width), F32),
             pltpu.VMEM((2, CHUNKS, ROWS, width), BF16),
             pltpu.VMEM((2, CHUNKS, AWAY, width), BF16),
             pltpu.VMEM((OWN, samples), F32),
@@ -455,6 +516,7 @@
             pltpu.SemaphoreType.DMA((2, 2)),
             pltpu.SemaphoreType.DMA((2, 2)),
             pltpu.SemaphoreType.DMA((2, 2)),
+            pltpu.SemaphoreType.REGULAR((3,)),
         ],
         compiler_params=pltpu.CompilerParams(
             collective_id=0, has_side_effects=True, vmem_limit_bytes=60 * 2**20

time: 62.7 us -> 60.9 us (0.971)
  Pallas kernels: 61.9 us -> 60.1 us
    pallas_call x1, Pallas kernels: 60.1 us -> 58.3 us  [shards(): pl.pallas_call(functools.partial(body, sizes), out_shape=(field, field, f...]
where the time goes in v4:
time: 60.9 us; the launch traced here: 60.7 us
  Pallas kernels  60.1 us (99%)
  between operations  0.64 us (1%)
    pallas_call x1, Pallas kernels, shards(): pl.pallas_call(functools.partial(body, sizes), out_shape=(field, field, f...  58.3 us
    pallas_call x1, Pallas kernels, shards(): pl.pallas_call(combine, out_shape=(shape, shape), in_specs=[vmem] * 4, ou...  1.79 us

profile of v4, /device:TPU:1, one launch (start us, length us, event | category | flops | bytes accessed | tf_op | source)
XLA Modules:
  0.0 60.7 jit_solution(1245228704163870495)
XLA Ops:
  0.6 58.3 %inversion.1 = (f32[64,512]{1,0:T(8,128)}, f32[64,512]{1,0:T(8,128)}, f32[64,512]{1,0:T(8,128)}, f32[8,128]{1,0:T(8,128)}) custom-call(bf16[128,512]{1,0:T(8,128)(2,1)} %traces_ref.1, bf16[8,512,512]{2,1,0:T(8,128)(2,1)} %kernels_ref.1, s32[1,4,4]{2,1,0:T(4,128)} %send_ref.1, s32[8,128]{1,0:T(8,128)} %slot_ref.1, s32[8,128]{1,0:T(8,128)} %pattern_ref.1, ...), custom_call_target="tpu_custom_call" | custom-call | tf_op jit(solution)/shard_map/inversion/pallas_call | solution.py:476
  58.9 1.8 %combine.1 = (f32[8,8,512]{2,1,0:T(8,128)}, f32[8,8,512]{2,1,0:T(8,128)}) custom-call(f32[64,512]{1,0:T(8,128)} %get-tuple-element.6.r_ref, f32[64,512]{1,0:T(8,128)} %get-tuple-element.7.z_ref, f32[64,512]{1,0:T(8,128)} %get-tuple-element.8.image_ref, f32[8,128]{1,0:T(8,128)} %get-tuple-element.9.weights_ref), custom_call_target="tpu_custom_call" | custom-call | tf_op jit(solution)/shard_map/combine/pallas_call | solution.py:527

commit v5 on v4

--- a/solution.py
+++ b/solution.py
@@ -194,17 +194,6 @@
         for j in range(APER):
             count = count + jnp.where(code[j : j + 1, :] - p * ROWS == row_id, 1.0, 0.0)
         spread_to[:, p * trace_rows : (p + 1) * trace_rows] = count.astype(BF16)
-        pick[p * trace_rows : (p + 1) * trace_rows, :] = count.T.astype(BF16)
-
-    entry = lax.broadcasted_iota(jnp.int32, (OWN, AWAY), 1)
-    listed = jnp.zeros((OWN, AWAY), jnp.int32)
-    for k in range(DIRS):
-        for m in range(SEND):
-            listed = jnp.where(entry // BINS == k * SEND + m, send_in[0, k : k + 1, m : m + 1], listed)
-    place = listed * BINS + entry % BINS
-    land_f32 = jnp.where(place == lax.broadcasted_iota(jnp.int32, (OWN, AWAY), 0), 1.0, 0.0)
-    land_at = land_f32.astype(BF16)
-    take_from = land_f32.T.astype(BF16)
 
     def cols(c):
         return slice(c * width, (c + 1) * width)
@@ -362,13 +351,10 @@
 
     lane = lax.broadcasted_iota(jnp.int32, (1, 128), 1)
 
-    def packed(parts):
-        out = jnp.zeros((1, 128), F32)
-        for i, part in enumerate(parts):
-            part = part + pltpu.roll(part, 64, 1)
-            part = part + pltpu.roll(part, 32, 1)
-            out = jnp.where(lane // 32 == i, part, out)
-        return out
+    def packed(row, i, part):
+        part = part + pltpu.roll(part, 64, 1)
+        part = part + pltpu.roll(part, 32, 1)
+        return jnp.where(lane // 32 == i, part, row)
 
     def unpacked(row, i):
         return jnp.sum(jnp.where(lane // 32 == i, row, 0.0), axis=1, keepdims=True)
@@ -382,6 +368,21 @@
     for c in range(CHUNKS):
         adjoint_chunk(0, c, values, first=True)
     meet(0)
+
+    for p in range(PATTERNS):
+        rows = slice(p * trace_rows, (p + 1) * trace_rows)
+        pick[rows, :] = spread_to[:, rows].astype(F32).T.astype(BF16)
+
+    entry = lax.broadcasted_iota(jnp.int32, (OWN, AWAY), 1)
+    listed = jnp.zeros((OWN, AWAY), jnp.int32)
+    for k in range(DIRS):
+        for m in range(SEND):
+            listed = jnp.where(entry // BINS == k * SEND + m, send_in[0, k : k + 1, m : m + 1], listed)
+    place = listed * BINS + entry % BINS
+    land_f32 = jnp.where(place == lax.broadcasted_iota(jnp.int32, (OWN, AWAY), 0), 1.0, 0.0)
+    land_at = land_f32.astype(BF16)
+    take_from = land_f32.T.astype(BF16)
+
     for c in range(CHUNKS):
         for p in range(PATTERNS):
             turned[c, :, p * width : (p + 1) * width] = moveout[p, cols(c), :].T
@@ -415,9 +416,12 @@
     stores[1].start()
     smooth[...] = smoothed(1, field1)
     cross = by_lanes(field1[...] * smooth[...])
+    sums = jnp.zeros((1, 128), F32)
+    for i, part in enumerate((curve_r, norm, norm_r)):
+        sums = packed(sums, i, part)
     met(2)
     heard = forward(1)
-    total_start(1, 0, packed((curve_r, norm, norm_r, by_lanes(heard * heard) + cross)))
+    total_start(1, 0, packed(sums, 3, by_lanes(heard * heard) + cross))
     for c in range(CHUNKS):
         fine_chunk(c, heard)
     total_start(1, 1, total_end(1, 0))

time: 60.9 us -> 60.7 us (level)
  no operation moved by 1% of the time
where the time goes in v5:
time: 60.7 us; the launch traced here: 60.6 us
  Pallas kernels  59.9 us (99%)
  between operations  0.64 us (1%)
    pallas_call x1, Pallas kernels, shards(): pl.pallas_call(functools.partial(body, sizes), out_shape=(field, field, f...  58.1 us
    pallas_call x1, Pallas kernels, shards(): pl.pallas_call(combine, out_shape=(shape, shape), in_specs=[vmem] * 4, ou...  1.79 us

profile of v5, /device:TPU:1, one launch (start us, length us, event | category | flops | bytes accessed | tf_op | source)
XLA Modules:
  0.0 60.6 jit_solution(8702391633745235816)
XLA Ops:
  0.6 58.1 %inversion.1 = (f32[64,512]{1,0:T(8,128)}, f32[64,512]{1,0:T(8,128)}, f32[64,512]{1,0:T(8,128)}, f32[8,128]{1,0:T(8,128)}) custom-call(bf16[128,512]{1,0:T(8,128)(2,1)} %traces_ref.1, bf16[8,512,512]{2,1,0:T(8,128)(2,1)} %kernels_ref.1, s32[1,4,4]{2,1,0:T(4,128)} %send_ref.1, s32[8,128]{1,0:T(8,128)} %slot_ref.1, s32[8,128]{1,0:T(8,128)} %pattern_ref.1, ...), custom_call_target="tpu_custom_call" | custom-call | tf_op jit(solution)/shard_map/inversion/pallas_call | solution.py:480
  58.8 1.8 %combine.1 = (f32[8,8,512]{2,1,0:T(8,128)}, f32[8,8,512]{2,1,0:T(8,128)}) custom-call(f32[64,512]{1,0:T(8,128)} %get-tuple-element.6.r_ref, f32[64,512]{1,0:T(8,128)} %get-tuple-element.7.z_ref, f32[64,512]{1,0:T(8,128)} %get-tuple-element.8.image_ref, f32[8,128]{1,0:T(8,128)} %get-tuple-element.9.weights_ref), custom_call_target="tpu_custom_call" | custom-call | tf_op jit(solution)/shard_map/combine/pallas_call | solution.py:531
